TPU v7x, 32 devices: a whole 2x2x4 slice. The times are simulated.
32 devices in a mesh: groups: 2 (over y), slab: 4 (over z), radar: 4 (over x, core).
Axes of the slice: x: 2, y: 2, z: 4, core: 2. Of those that a mesh axis runs over, the one named last changes fastest.
Arguments:
- wind: float32 [8, 2048, 2, 2048], P(('groups', 'radar'), 'slab'), parts along dimension 0, may hold values from -6 to 6
- obs_velocity: float32 [16384, 128], P(('groups', 'slab', 'radar')), parts along dimension 0, may hold values from -6 to 6
- gate_weight: float32 [16384, 128], P(('groups', 'slab', 'radar')), parts along dimension 0, may hold values from 0.1 to 1
- azimuth: float32 [16384, 128], P(('groups', 'slab', 'radar')), parts along dimension 0, may hold values from -3.140625 to 3.140625
- block_owner: int32 [16384, 1], P(('groups', 'slab', 'radar')), parts along dimension 0, may hold values from 0 to 3; in each aligned block of 512 rows (0 to 511, 512 to 1023, ...) at most 256 rows name the same one
- block_cell: int32 [16384], P(('groups', 'slab', 'radar')), parts along dimension 0, may hold values from 0 to 1048575
Outputs:
- updated_wind: float32 [8, 2048, 2, 2048], P(('groups', 'radar'), 'slab'), parts along dimension 0
- total_cost: float32 [2], P('groups'), parts along dimension 0
There are 2 independent parts, one for each index of `groups`. A program takes and returns all parts, laid end to end along the dimension named above; each array names one. Nothing has to cross between parts.
Inputs may be any that keep to these rules, and one draw needn't show every extreme that they name: `block_owner`: among the 512 blocks of one device at most 256 name the same owner, and in every draw some owner is named by exactly 256 of them.
All inputs are finite; a program needn't handle non-finite values.
Results may differ from a plain program's by a relative error of at most 0.0017.
The roundings to bfloat16 on the way count: a program that leaves them out, or rounds other values in their place, can miss the bound.
Values may be sent and summed in bfloat16 or wider, within the bound.
A program may use at most 128 MiB of HBM per device.

v0:
```python
import math

import jax
import jax.numpy as jnp
from jax import lax
from jax.sharding import PartitionSpec as P

divergence_weight = 2.0
spectral_shift = 0.0001


def extended_2(cells, sides, width):
    for axis, dim in sides:
        count = lax.axis_size(axis)
        ends = count - 1
        head = lax.slice_in_dim(cells, 0, width, axis=dim)
        tail = lax.slice_in_dim(cells, cells.shape[dim] - width, cells.shape[dim], axis=dim)
        cells = jnp.concatenate(
            [
                lax.ppermute(tail, axis, [(i, (i + 1) % count) for i in range(ends)]),
                cells,
                lax.ppermute(head, axis, [((i + 1) % count, i) for i in range(ends)]),
            ],
            axis=dim,
        )
    return cells


def dst_table(length):
    rows = lax.iota(jnp.int32, length) + 1
    phase = rows[:, None] * rows[None, :] % (2 * (length + 1))
    angle = math.pi / (length + 1) * phase.astype(jnp.float32)
    return (math.sqrt(2.0 / (length + 1)) * jnp.sin(angle)).astype(jnp.bfloat16)


def eigen_values(length, start, count):
    waves = (start + lax.iota(jnp.int32, count) + 1).astype(jnp.float32)
    return 4.0 * jnp.sin(math.pi / (2 * (length + 1)) * waves) ** 2


def gate_terms(observed, weight, angle, u_val, v_val):
    cosine = jnp.cos(angle)
    sine = jnp.sin(angle)
    misfit = weight * (cosine * u_val + sine * v_val) - observed
    cost = 0.5 * jnp.sum(misfit * misfit)
    part_u = jnp.sum(weight * cosine * misfit, axis=-1)
    part_v = jnp.sum(weight * sine * misfit, axis=-1)
    return (cost, part_u, part_v)


def y_diff(field):
    padded = jnp.pad(field, ((0, 0), (1, 1)))
    return padded[:, 2:] - padded[:, :-2]


def local(wind, obs_velocity, gate_weight, azimuth, block_owner, block_cell):
    slabs = lax.axis_size("slab")
    here = lax.axis_index("slab")
    field = wind[0]
    width_x, _, width_y = field.shape
    total_x = width_x * slabs
    part_y = width_y // slabs
    blocks, gates = obs_velocity.shape
    capacity = 2 * blocks // slabs
    owner = block_owner[:, 0]
    match = (owner[:, None] == lax.iota(jnp.int32, slabs)[None, :]).astype(jnp.int32)
    before = jnp.cumsum(match, axis=0) - match
    rank = jnp.sum(before * match, axis=1)
    slot = owner * capacity + rank
    flat = field.reshape(-1)
    grad_flat = jnp.zeros((width_x * 2 * width_y,), jnp.float32)
    obs_buf = jnp.zeros((slabs * capacity, gates), jnp.float32).at[slot].set(obs_velocity)
    weight_buf = jnp.zeros((slabs * capacity, gates), jnp.float32).at[slot].set(gate_weight)
    angle_buf = jnp.zeros((slabs * capacity, gates), jnp.float32).at[slot].set(azimuth)
    cell_buf = jnp.full((slabs * capacity,), -1, jnp.int32).at[slot].set(block_cell)
    got_obs, got_weight, got_angle, got_cell = (
        lax.all_to_all(obs_buf, "slab", split_axis=0, concat_axis=0, tiled=True),
        lax.all_to_all(weight_buf, "slab", split_axis=0, concat_axis=0, tiled=True),
        lax.all_to_all(angle_buf, "slab", split_axis=0, concat_axis=0, tiled=True),
        lax.all_to_all(cell_buf, "slab", split_axis=0, concat_axis=0, tiled=True),
    )
    safe = jnp.maximum(got_cell, 0)
    index_u = safe // width_y * (2 * width_y) + safe % width_y
    cost_obs, part_u, part_v = gate_terms(
        got_obs, got_weight, got_angle, flat[index_u][:, None], flat[index_u + width_y][:, None]
    )
    grad_flat = grad_flat.at[index_u].add(part_u).at[index_u + width_y].add(part_v)
    grad_obs = grad_flat.reshape(width_x, 2, width_y)
    extended = extended_2(field, (("slab", 0),), 1)
    div = 0.5 * (extended[2:, 0] - extended[:-2, 0]) + 0.5 * y_diff(field[:, 1])
    div_ext = extended_2(div, (("slab", 0),), 1)
    cost_div = 0.5 * divergence_weight * jnp.sum(div * div)
    local_cost = cost_obs + cost_div
    grad_u = divergence_weight * 0.5 * (div_ext[:-2] - div_ext[2:])
    padded_div = jnp.pad(div, ((0, 0), (1, 1)))
    grad_v = divergence_weight * 0.5 * (padded_div[:, :-2] - padded_div[:, 2:])
    gradient = grad_obs + jnp.stack([grad_u, grad_v], axis=1)
    cost_total = lax.psum(local_cost, ("slab", "radar"))
    table_y = dst_table(width_y)
    table_x = dst_table(total_x)
    lowered = gradient.astype(jnp.bfloat16)
    spec_y = jnp.einsum("xcy,yk->xck", lowered, table_y, preferred_element_type=jnp.float32).astype(
        jnp.bfloat16
    )
    columns = lax.all_to_all(spec_y, "slab", split_axis=2, concat_axis=0, tiled=True)
    spec = jnp.dot(
        table_x, columns.reshape(total_x, 2 * part_y), preferred_element_type=jnp.float32
    )
    spec = spec.reshape(total_x, 2, part_y)
    eig = (
        eigen_values(total_x, 0, total_x)[:, None, None]
        + eigen_values(width_y, here * part_y, part_y)[None, None, :]
        + spectral_shift
    )
    scaled = spec / eig
    energy_part = jnp.sum(spec * scaled)
    energy = lax.psum(energy_part, ("slab", "radar"))
    back_x = jnp.dot(
        table_x,
        scaled.astype(jnp.bfloat16).reshape(total_x, 2 * part_y),
        preferred_element_type=jnp.float32,
    )
    back_x = back_x.astype(jnp.bfloat16).reshape(total_x, 2, part_y)
    rows = lax.all_to_all(back_x, "slab", split_axis=0, concat_axis=2, tiled=True)
    precond = jnp.einsum("xck,ky->xcy", rows, table_y, preferred_element_type=jnp.float32)
    updated = field - cost_total / energy * precond
    return (updated[None], jnp.reshape(cost_total, (1,)))


def solution(mesh):
    return jax.shard_map(
        local,
        mesh=mesh,
        in_specs=(
            P(("groups", "radar"), "slab", None, None),
            P(("groups", "slab", "radar"), None),
            P(("groups", "slab", "radar"), None),
            P(("groups", "slab", "radar"), None),
            P(("groups", "slab", "radar"), None),
            P(("groups", "slab", "radar")),
        ),
        out_specs=(P(("groups", "radar"), "slab", None, None), P("groups")),
        check_vma=False,
    )
```

profile of v0, /device:TPU:0, one launch (start us, length us, event | category | flops | bytes accessed | tf_op | source)
XLA Modules:
  0.0 683.8 jit_solution(3571143749141522073)
XLA Ops:
  20.5 8.2 %copy.55 = f32[1,512,2,2048]{3,1,2,0:T(8,128)S(1)} copy(f32[1,512,2,2048]{3,2,1,0:T(2,128)} %param.6) | data formatting | bytes 16777216 | tf_op args[0]
  54.1 13.3 %all-to-all-done.1 = f32[4,256,128]{2,1,0:T(8,128)S(1)} async-done(((f32[4,256,128]{2,1,0:T(8,128)}), f32[4,256,128]{2,1,0:T(8,128)S(1)}, u32[]{:S(2)}, u32[]{:S(2)}) %all-to-all-start.1) | async-done | bytes 524320 | tf_op jit(solution)/shard_map/all_to_all | solution.py:79
  70.9 9.4 %multiply_reduce_fusion.1 = (f32[]{:T(128)}, f32[512,2048]{1,0:T(8,128)S(1)}) fusion(f32[512,2048]{1,0:T(8,128)} %slice_bitcast_fusion, f32[512,2,2048]{2,0,1:T(8,128)} %bitcast.114, f32[1,2,2048]{2,0,1:T(1,128)S(1)} %collective-permute-done.1, f32[1,2,2048]{2,0,1:T(1,128)S(1)} %collective-permute-done), kind=kLoop, calls=%fused_computation.53 | loop fusion | flops 8388607 | bytes 16809988 | tf_op jit(solution)/shard_map/reduce_sum | solution.py:92
  93.2 13.6 %gather_fusion.1 = f32[1024]{0:T(1024)S(1)} fusion(f32[2097152]{0:T(1024)} %bitcast.116, s32[1024]{0:T(1024)S(1)} %broadcast_clamp_fusion), kind=kCustom, calls=%fused_computation.1 | custom fusion | bytes 12288 | tf_op jit(solution)/shard_map/gather | solution.py:85
  106.7 13.6 %gather_fusion = f32[1024]{0:T(1024)S(1)} fusion(f32[2097152]{0:T(1024)} %bitcast.117, s32[1024]{0:T(1024)S(1)} %broadcast_clamp_fusion.1), kind=kCustom, calls=%fused_computation | custom fusion | bytes 12288 | tf_op jit(solution)/shard_map/gather | solution.py:85
  120.3 11.5 %fusion.27 = (f32[512,1,2048]{2,0,1:T(8,128)}, f32[512,1,2048]{2,0,1:T(8,128)}) fusion(f32[1,2048]{1,0:T(1,128)S(1)} %collective-permute-done.3, f32[512,2048]{1,0:T(8,128)} %copy-done.2, f32[1,2048]{1,0:T(1,128)S(1)} %collective-permute-done.2), kind=kLoop, calls=%fused_computation.42 | loop fusion | flops 4194304 | bytes 12599296 | tf_op jit(solution)/shard_map/stack | solution.py:97
  134.9 9.8 %scatter_custom_fusion.4 = f32[2097152]{0:T(1024)} fusion(s32[1024]{0:T(1024)S(1)} %bitcast.133, f32[1024]{0:T(1024)S(1)} %bitcast.139, f32[]{:T(128)} %constant.73.clone.1), kind=kCustom, calls=%fused_computation.51 | custom fusion | flops 1024 | bytes 8388612 | tf_op jit(solution)/shard_map/scatter-add | solution.py:87
  144.7 12.2 %scatter_fusion = f32[2097152]{0:T(1024)} fusion(f32[2097152]{0:T(1024)} %scatter_custom_fusion.4, s32[1024]{0:T(1024)S(1)} %bitcast.124, f32[1024]{0:T(1024)S(1)} %bitcast.127), kind=kCustom, calls=%fused_computation.7 | custom fusion | flops 1024 | bytes 16384 | tf_op jit(solution)/shard_map/scatter-add | solution.py:87
  156.9 10.7 %reshape.228 = f32[512,2,2048]{2,1,0:T(2,128)} reshape(f32[2097152]{0:T(1024)} %scatter_fusion) | data formatting | bytes 16777216 | tf_op jit(solution)/shard_map/reshape | solution.py:88
  167.7 10.4 %fusion.98 = bf16[512,2,2048]{2,0,1:T(8,128)(2,1)S(1)} fusion(f32[512,1,2048]{2,0,1:T(8,128)} %get-tuple-element.22, f32[512,1,2048]{2,0,1:T(8,128)} %get-tuple-element.21, f32[512,2,2048]{2,1,0:T(2,128)} %reshape.228), kind=kLoop, calls=%fused_computation.19.clone.clone.clone.clone.2 | loop fusion | flops 6291456 | bytes 20971520 | tf_op jit(solution)/shard_map/xcy,yk->xck/dot_general | solution.py:102
  178.1 83.8 %fusion.37 = bf16[512,2,2048]{2,0,1:T(8,128)(2,1)} fusion(s32[2048]{0:T(1024)S(1)} %iota_add_fusion, bf16[512,2,2048]{2,0,1:T(8,128)(2,1)S(1)} %fusion.98), kind=kOutput, calls=%fused_computation.55 | convolution fusion | flops 8638169088 | bytes 8396800 | tf_op jit(solution)/shard_map/xcy,yk->xck/dot_general | solution.py:102
  261.9 11.1 %copy.26 = bf16[512,2,2048]{0,1,2:T(2,128)(2,1)} copy(bf16[512,2,2048]{2,0,1:T(8,128)(2,1)} %fusion.37) | data formatting | bytes 8388608 | tf_op jit(solution)/shard_map/convert_element_type | solution.py:102
  273.0 54.2 %all-to-all-start.4 = ((bf16[512,2,2048]{0,1,2:T(2,128)(2,1)}), bf16[512,2,2048]{0,1,2:T(2,128)(2,1)}, u32[]{:S(2)}, u32[]{:S(2)}) async-start(bf16[512,2,2048]{0,1,2:T(2,128)(2,1)} %copy.26), calls=%async_computation.4 | async-start | bytes 8388608 | tf_op jit(solution)/shard_map/all_to_all | solution.py:105
  329.7 66.2 %fusion.12.clone.4 = bf16[2048,2048,1]{1,0,2:T(8,128)(2,1)} fusion(s32[2048]{0:T(1024)S(1)} %iota_add_fusion), kind=kLoop, calls=%fused_computation.23.clone.clone.clone.1 | loop fusion | flops 46137344 | bytes 8396800 | tf_op jit(solution)/shard_map/convert_element_type | solution.py:120
  395.9 66.2 %fusion.96 = bf16[2048,2048]{1,0:T(8,128)(2,1)} fusion(s32[2048]{0:T(1024)S(1)} %iota_add_fusion), kind=kLoop, calls=%fused_computation.13.clone.2.clone.clone.clone.1 | loop fusion | flops 46137344 | bytes 8396800 | tf_op jit(solution)/shard_map/dot_general | solution.py:118
  462.1 19.9 %copy.27 = bf16[512,2,4,512]{3,1,0,2:T(2,128)(2,1)} copy(bf16[512,2,4,512]{0,1,3,2:T(2,128)(2,1)} %bitcast.22) | data formatting | bytes 8388608 | tf_op jit(solution)/shard_map/all_to_all | solution.py:105
  493.9 14.5 %divide_convert_fusion = (bf16[2048,2,512]{0,2,1:T(8,128)(2,1)S(1)}, f32[]{:T(128)}) fusion(f32[2048,512]{0,1:T(8,128)} %add_add_fusion, bf16[2,512,2048]{2,1,0:T(8,128)(2,1)} %bitcast.121, bf16[2048,2048,1]{1,0,2:T(8,128)(2,1)} %fusion.12.clone.4), kind=kOutput, calls=%fused_computation.30 | convolution fusion | flops 8598323200 | bytes 20971524 | tf_op jit(solution)/shard_map/dot_general | solution.py:106
  508.3 12.6 %fusion.34 = bf16[2048,1024]{0,1:T(8,128)(2,1)} fusion(bf16[2048,1024]{0,1:T(8,128)(2,1)S(1)} %bitcast.144, bf16[2048,2048]{1,0:T(8,128)(2,1)} %fusion.96), kind=kOutput, calls=%fused_computation.54 | convolution fusion | flops 8592031744 | bytes 16777216 | tf_op jit(solution)/shard_map/dot_general | solution.py:118
  520.9 11.1 %copy.29 = bf16[2048,2,512]{2,1,0:T(2,128)(2,1)} copy(bf16[2048,2,512]{0,2,1:T(8,128)(2,1)} %bitcast.122) | data formatting | bytes 8388608 | tf_op jit(solution)/shard_map/reshape | solution.py:123
  537.1 66.2 %fusion.93 = bf16[2048,2048,1]{1,0,2:T(8,128)(2,1)} fusion(s32[2048]{0:T(1024)S(1)} %iota_add_fusion), kind=kLoop, calls=%fused_computation.21.clone.clone.clone.1 | loop fusion | flops 46137344 | bytes 8396800 | tf_op jit(solution)/shard_map/xck,ky->xcy/dot_general | solution.py:125
  604.6 35.0 %all-reduce.2 = (f32[]{:T(128)}, f32[]{:T(128)}) all-reduce(f32[]{:T(128)S(6)} %add.217, f32[]{:T(128)} %get-tuple-element.18), channel_id=1, replica_groups=mesh['groups'=2,'slab'=4,'radar'=4] {'slab','radar'}, use_global_device_ids=true, to_apply=%region_9.10 | all-reduce | flops 2 | bytes 16 | tf_op jit(solution)/shard_map/psum | solution.py:98
  648.2 7.7 %all_to_all.62 = bf16[512,2,2048]{2,0,1:T(8,128)(2,1)} reshape(bf16[512,2,4,512]{3,2,0,1:T(4,128)(2,1)} %bitcast.120) | data formatting | bytes 8388608 | tf_op jit(solution)/shard_map/all_to_all | solution.py:124
  656.0 16.5 %subtract_bitcast_fusion = f32[1,512,2,2048]{3,1,2,0:T(8,128)S(1)} fusion(f32[]{:T(128)S(6)} %div.26, bf16[512,2,2048]{2,0,1:T(8,128)(2,1)} %all_to_all.62, f32[1,512,2,2048]{3,2,1,0:T(2,128)} %param.6, bf16[2048,2048,1]{1,0,2:T(8,128)(2,1)} %fusion.93), kind=kOutput, calls=%fused_computation.27 | convolution fusion | flops 8594128896 | bytes 29360132 | tf_op jit(solution)/shard_map/xck,ky->xcy/dot_general | solution.py:125
  672.5 11.1 %copy.31 = f32[1,512,2,2048]{3,2,1,0:T(2,128)} copy(f32[1,512,2,2048]{3,1,2,0:T(8,128)S(1)} %subtract_bitcast_fusion) | data formatting | bytes 16777216
  (60 shorter events, 91.3 us)
Async XLA Ops:
  7.6 42.2 %all-to-all-start.2 = ((s32[4,256,1]{1,2,0:T(1,128)}), s32[4,256,1]{1,2,0:T(1,128)S(1)}, u32[]{:S(2)}, u32[]{:S(2)}) async-start(s32[4,256,1]{1,2,0:T(1,128)} %bitcast.8), calls=%async_computation.2 | async-start | bytes 8192 | tf_op jit(solution)/shard_map/all_to_all | solution.py:80
  14.6 56.3 %collective-permute-start = (f32[1,2,2048]{2,0,1:T(1,128)S(1)}, f32[1,2,2048]{2,0,1:T(1,128)S(1)}, u32[]{:S(2)}, u32[]{:S(2)}) collective-permute-start(f32[1,2,2048]{2,0,1:T(1,128)S(1)} %bitcast.135), channel_id=1, source_target_pairs={{4,0},{8,4},{12,8},{5,1},{9,5},{13,9},{6,2},{10,6},{14,10},{7,3},{... | collective-permute-start | bytes 49160 | tf_op jit(solution)/shard_map/ppermute | solution.py:22
  16.0 54.9 %collective-permute-start.1 = (f32[1,2,2048]{2,0,1:T(1,128)S(1)}, f32[1,2,2048]{2,0,1:T(1,128)S(1)}, u32[]{:S(2)}, u32[]{:S(2)}) collective-permute-start(f32[1,2,2048]{2,0,1:T(1,128)S(1)} %bitcast.136), channel_id=1, source_target_pairs={{0,4},{4,8},{8,12},{1,5},{5,9},{9,13},{2,6},{6,10},{10,14},{3,7},{... | collective-permute-start | bytes 49160 | tf_op jit(solution)/shard_map/ppermute | solution.py:20
  28.8 4.3 copy-start
  28.8 7.9 %copy-start.1 = (f32[1,512,2,2048]{3,2,1,0:T(2,128)S(1)}, f32[1,512,2,2048]{3,2,1,0:T(2,128)}, u32[]{:S(2)}) copy-start(f32[1,512,2,2048]{3,2,1,0:T(2,128)} %param.6) | copy-start | bytes 25165828
  49.8 17.6 %all-to-all-start.1 = ((f32[4,256,128]{2,1,0:T(8,128)}), f32[4,256,128]{2,1,0:T(8,128)S(1)}, u32[]{:S(2)}, u32[]{:S(2)}) async-start(f32[4,256,128]{2,1,0:T(8,128)} %bitcast.7), calls=%async_computation.1 | async-start | bytes 1048576 | tf_op jit(solution)/shard_map/all_to_all | solution.py:79
  67.4 20.0 %all-to-all-start = ((f32[4,256,128]{2,1,0:T(8,128)}), f32[4,256,128]{2,1,0:T(8,128)S(1)}, u32[]{:S(2)}, u32[]{:S(2)}) async-start(f32[4,256,128]{2,1,0:T(8,128)} %bitcast.6), calls=%async_computation | async-start | bytes 1048576 | tf_op jit(solution)/shard_map/all_to_all | solution.py:78
  80.3 1.9 copy-start.2
  82.2 38.1 %collective-permute-start.2 = (f32[1,2048]{1,0:T(1,128)S(1)}, f32[1,2048]{1,0:T(1,128)S(1)}, u32[]{:S(2)}, u32[]{:S(2)}) collective-permute-start(f32[1,2048]{1,0:T(1,128)S(1)} %get-tuple-element.23), channel_id=1, source_target_pairs={{0,4},{4,8},{8,12},{1,5},{5,9},{9,13},{2,6},{6,10},{10,14},{3,7},{... | collective-permute-start | bytes 24584 | tf_op jit(solution)/shard_map/ppermute | solution.py:20
  86.1 34.2 %collective-permute-start.3 = (f32[1,2048]{1,0:T(1,128)S(1)}, f32[1,2048]{1,0:T(1,128)S(1)}, u32[]{:S(2)}, u32[]{:S(2)}) collective-permute-start(f32[1,2048]{1,0:T(1,128)S(1)} %get-tuple-element.24), channel_id=1, source_target_pairs={{4,0},{8,4},{12,8},{5,1},{9,5},{13,9},{6,2},{10,6},{14,10},{7,3},{... | collective-permute-start | bytes 24584 | tf_op jit(solution)/shard_map/ppermute | solution.py:22
  87.4 46.3 %all-to-all-start.3 = ((f32[4,256,128]{2,1,0:T(8,128)}), f32[4,256,128]{2,1,0:T(8,128)S(1)}, u32[]{:S(2)}, u32[]{:S(2)}) async-start(f32[4,256,128]{2,1,0:T(8,128)} %bitcast.14), calls=%async_computation.3 | async-start | bytes 1048576 | tf_op jit(solution)/shard_map/all_to_all | solution.py:77
  273.0 189.1 %all-to-all-start.4 = ((bf16[512,2,2048]{0,1,2:T(2,128)(2,1)}), bf16[512,2,2048]{0,1,2:T(2,128)(2,1)}, u32[]{:S(2)}, u32[]{:S(2)}) async-start(bf16[512,2,2048]{0,1,2:T(2,128)(2,1)} %copy.26), calls=%async_computation.4 | async-start | bytes 8388608 | tf_op jit(solution)/shard_map/all_to_all | solution.py:105
  532.0 108.8 %all-to-all-start.5 = ((bf16[2048,2,512]{2,1,0:T(2,128)(2,1)}), bf16[2048,2,512]{2,1,0:T(2,128)(2,1)}, u32[]{:S(2)}, u32[]{:S(2)}) async-start(bf16[2048,2,512]{2,1,0:T(2,128)(2,1)} %copy.29), calls=%async_computation.5 | async-start | bytes 8388608 | tf_op jit(solution)/shard_map/all_to_all | solution.py:124
where the time goes:
time: 696 us; the launch traced here: 684 us
  other arithmetic  259 us (37%)
  local copies, waits for them, and re-layouts  155 us (22%)
  matrix products  127 us (18%)
  starting transfers between devices  90 us (13%)
  blocking collectives  35 us (5%)
  waiting for transfers between devices  13.4 us (2%)
    dot_general x1, matrix products, local(): jnp.einsum('xcy,yk->xck', lowered, table_y, preferred_element_type=jnp.fl...  83.8 us
    dot_general x1, other arithmetic, local(): jnp.dot(table_x, scaled.astype(jnp.bfloat16).reshape(total_x, 2 * part_y)...  66.2 us
    convert_element_type x1, other arithmetic, local(): scaled.astype(jnp.bfloat16).reshape(total_x, 2 * part_y)  66.2 us
    dot_general x1, other arithmetic, local(): jnp.einsum('xck,ky->xcy', rows, table_y, preferred_element_type=jnp.float32)  66.2 us
    all_to_all x1, starting transfers between devices, local(): lax.all_to_all(spec_y, 'slab', split_axis=2, concat_axis=0, tiled=True)  54.2 us
    unnamed x14, local copies, waits for them, and re-layouts  36.5 us
    psum x1, blocking collectives, local(): cost_total = lax.psum(local_cost, ('slab', 'radar'))  35 us
    scatter-add x2, other arithmetic, local(): grad_flat.at[index_u].add(part_u).at[index_u + width_y].add(part_v)  22.1 us
  transfers between devices with their start and end apart: 10, of which 1 were waited for; matrix products, arithmetic and copies ran while one was open for 40% of the time, Pallas kernels for 0%

commit v1 on v0

v1 whole, which is shorter than its diff:
```python
import functools
import math

import jax
import jax.numpy as jnp
from jax import lax
from jax.experimental import pallas as pl
from jax.experimental.pallas import tpu as pltpu
from jax.sharding import PartitionSpec as P

divergence_weight = 2.0
spectral_shift = 0.0001
vmem_bytes = 56 * 1024 * 1024
halo = 8


def dst_table(length):
    inner = math.gcd(length, 64)
    outer = length // inner
    waves = lax.iota(jnp.int32, length) + 1
    period = 2 * (length + 1)
    scale = math.sqrt(2.0 / (length + 1))

    def angles(steps):
        phase = steps[:, None] * waves[None, :] % period
        return math.pi / (length + 1) * phase.astype(jnp.float32)

    coarse = angles(lax.iota(jnp.int32, outer) * inner)
    fine = angles(lax.iota(jnp.int32, inner) + 1)
    coarse_s, coarse_c, fine_s, fine_c = lax.optimization_barrier(
        (scale * jnp.sin(coarse), scale * jnp.cos(coarse), jnp.sin(fine), jnp.cos(fine))
    )
    table = coarse_s[:, None, :] * fine_c[None] + coarse_c[:, None, :] * fine_s[None]
    return table.astype(jnp.bfloat16).reshape(length, length)


def eigen_values(length, start, count):
    waves = (start + lax.iota(jnp.int32, count) + 1).astype(jnp.float32)
    return 4.0 * jnp.sin(math.pi / (2 * (length + 1)) * waves) ** 2


def gradient_kernel(ends, cell_ref, coef_ref, wind_ref, out_ref, cost_ref, grad_ref, sum_ref):
    _, rows, width = out_ref.shape
    slabs, _, capacity = coef_ref.shape
    here = lax.axis_index("slab")
    step = min(32, rows)
    tall = step + 2 * halo

    sum_ref[...] = jnp.zeros_like(sum_ref)
    lane = lax.broadcasted_iota(jnp.int32, (tall, width), 1)
    row = lax.broadcasted_iota(jnp.int32, (tall, width), 0)

    def y_sides(field):
        before = jnp.where(lane == 0, 0.0, pltpu.roll(field, 1, 1))
        after = jnp.where(lane == width - 1, 0.0, pltpu.roll(field, width - 1, 1))
        return before, after

    def stencil(i, carry):
        start = pl.multiple_of(i * step, 8)
        u = wind_ref[0, pl.ds(start, tall), :]
        v = wind_ref[1, pl.ds(start, tall), :]
        before, after = y_sides(v)
        div = 0.5 * (pltpu.roll(u, tall - 1, 0) - pltpu.roll(u, 1, 0)) + 0.5 * (after - before)
        place = here * rows + start - halo + row
        div = jnp.where((place >= 0) & (place < ends), div, 0.0)
        kept = div[halo : halo + step]
        sum_ref[...] += jnp.sum((kept * kept).reshape(step // 8, 8, width), axis=0)
        grad_u = pltpu.roll(div, 1, 0) - pltpu.roll(div, tall - 1, 0)
        before, after = y_sides(div)
        grad_v = before - after
        scale = divergence_weight * 0.5
        grad_ref[0, pl.ds(start, step), :] = scale * grad_u[halo : halo + step]
        grad_ref[1, pl.ds(start, step), :] = scale * grad_v[halo : halo + step]
        return carry

    lax.fori_loop(0, rows // step, stencil, 0)

    spot = lax.broadcasted_iota(jnp.int32, (8, 128), 0) * 128
    spot = spot + lax.broadcasted_iota(jnp.int32, (8, 128), 1)

    def gate_block(s, i, total):
        cell = cell_ref[s, i]
        x = cell // width
        y = cell - x * width
        top = pl.multiple_of(x // 8 * 8, 8)
        first = pl.multiple_of(y // 128 * 128, 128)
        mask = spot == (x - top) * 128 + (y - first)
        u = wind_ref[0, pl.ds(pl.multiple_of(top + halo, 8), 8), pl.ds(first, 128)]
        v = wind_ref[1, pl.ds(pl.multiple_of(top + halo, 8), 8), pl.ds(first, 128)]
        uu, uv, vv = coef_ref[s, 0, i], coef_ref[s, 1, i], coef_ref[s, 2, i]
        ou, ov = coef_ref[s, 3, i], coef_ref[s, 4, i]
        part_u = uu * u + uv * v - ou
        part_v = uv * u + vv * v - ov
        grad_ref[0, pl.ds(top, 8), pl.ds(first, 128)] += jnp.where(mask, part_u, 0.0)
        grad_ref[1, pl.ds(top, 8), pl.ds(first, 128)] += jnp.where(mask, part_v, 0.0)
        return total + jnp.where(mask, u * (part_u - ou) + v * (part_v - ov), 0.0)

    def gate_group(t, total):
        s = t // (capacity // 8)
        base = (t - s * (capacity // 8)) * 8
        for k in range(8):
            total = gate_block(s, base + k, total)
        return total

    total = lax.fori_loop(
        0, slabs * capacity // 8, gate_group, jnp.zeros((8, 128), jnp.float32)
    )
    cost_div = 0.5 * divergence_weight * jnp.sum(sum_ref[...], keepdims=True)
    cost_ref[...] = cost_div + 0.5 * jnp.sum(total, keepdims=True)

    def lower(i, carry):
        at = pl.ds(pl.multiple_of(i * step, 16), step)
        out_ref[0, at, :] = grad_ref[0, at, :].astype(jnp.bfloat16)
        out_ref[1, at, :] = grad_ref[1, at, :].astype(jnp.bfloat16)
        return carry

    lax.fori_loop(0, rows // step, lower, 0)


def y_forward_kernel(grad_ref, table_ref, out_ref):
    parts, _, part = out_ref.shape
    spec = jnp.dot(grad_ref[0], table_ref[...], preferred_element_type=jnp.float32)
    spec = spec.astype(jnp.bfloat16)
    for d in range(parts):
        out_ref[d] = spec[:, d * part : (d + 1) * part]


def x_kernel(cols_ref, table_ref, lam_x_ref, lam_y_ref, out_ref, energy_ref, scaled_ref):
    phase, i = pl.program_id(0), pl.program_id(1)
    slabs, rows, part = cols_ref.shape
    block = table_ref.shape[0]

    @pl.when((phase == 0) & (i == 0))
    def _():
        energy_ref[...] = jnp.zeros_like(energy_ref)

    @pl.when(phase == 0)
    def _():
        cols = cols_ref[...].reshape(slabs * rows, part)
        spec = jnp.dot(table_ref[...], cols, preferred_element_type=jnp.float32)
        scaled = spec / (lam_x_ref[...] + lam_y_ref[...] + spectral_shift)
        energy_ref[...] += jnp.sum((spec * scaled).reshape(block // 8, 8, part), axis=0)
        scaled_ref[pl.ds(pl.multiple_of(i * block, block), block), :] = scaled.astype(jnp.bfloat16)

    @pl.when(phase == 1)
    def _():
        back = jnp.dot(table_ref[...], scaled_ref[...], preferred_element_type=jnp.float32)
        out_ref[...] = back.astype(jnp.bfloat16).reshape(out_ref.shape)


def y_back_kernel(rows_ref, table_ref, out_ref, held_ref):
    slabs, _, part = rows_ref.shape

    @pl.when(pl.program_id(0) == 0)
    def _():
        for d in range(slabs):
            held_ref[:, d * part : (d + 1) * part] = rows_ref[d]

    out_ref[...] = jnp.dot(held_ref[...], table_ref[...], preferred_element_type=jnp.float32)


def whole(shape):
    return pl.BlockSpec(shape, lambda *_: (0,) * len(shape))


def cost_of(flops, moved):
    return pl.CostEstimate(flops=flops, bytes_accessed=moved, transcendentals=0)


def params(steps):
    return pltpu.CompilerParams(
        vmem_limit_bytes=vmem_bytes, dimension_semantics=("arbitrary",) * steps
    )


def gradient_of(cells, coefs, wind_ext, rows, ends):
    _, tall, width = wind_ext.shape
    smem = pl.BlockSpec(memory_space=pltpu.SMEM)
    vmem = pl.BlockSpec(memory_space=pltpu.VMEM)
    return pl.pallas_call(
        functools.partial(gradient_kernel, ends),
        out_shape=(
            jax.ShapeDtypeStruct((2, rows, width), jnp.bfloat16),
            jax.ShapeDtypeStruct((1, 1), jnp.float32),
        ),
        in_specs=[smem, smem, vmem],
        out_specs=(vmem, vmem),
        scratch_shapes=[
            pltpu.VMEM((2, rows, width), jnp.float32),
            pltpu.VMEM((8, width), jnp.float32),
        ],
        compiler_params=pltpu.CompilerParams(vmem_limit_bytes=vmem_bytes),
        cost_estimate=cost_of(60 * rows * width, 12 * rows * width),
        name="gradient",
    )(cells, coefs, wind_ext)


def y_forward(grad, component, table, slabs):
    _, rows, width = grad.shape
    part = width // slabs
    block = max(part, min(512, width))
    return pl.pallas_call(
        y_forward_kernel,
        grid=(width // block,),
        out_shape=jax.ShapeDtypeStruct((slabs, rows, part), jnp.bfloat16),
        in_specs=[
            pl.BlockSpec((1, rows, width), lambda j: (component, 0, 0)),
            pl.BlockSpec((width, block), lambda j: (0, j)),
        ],
        out_specs=pl.BlockSpec((block // part, rows, part), lambda j: (j, 0, 0)),
        compiler_params=params(1),
        cost_estimate=cost_of(2 * rows * width * width, 2 * width * (width + 2 * rows)),
        name="y_forward",
    )(grad, table)


def x_transforms(cols, table, lam_x, lam_y):
    slabs, rows, part = cols.shape
    length = slabs * rows
    block = max(rows, min(512, length))
    return pl.pallas_call(
        x_kernel,
        grid=(2, length // block),
        out_shape=(
            jax.ShapeDtypeStruct((slabs, rows, part), jnp.bfloat16),
            jax.ShapeDtypeStruct((8, part), jnp.float32),
        ),
        in_specs=[
            whole((slabs, rows, part)),
            pl.BlockSpec((block, length), lambda p, i: (i, 0)),
            pl.BlockSpec((block, 1), lambda p, i: (i, 0)),
            whole((1, part)),
        ],
        out_specs=(
            pl.BlockSpec((block // rows, rows, part), lambda p, i: (p * i, 0, 0)),
            whole((8, part)),
        ),
        scratch_shapes=[pltpu.VMEM((length, part), jnp.bfloat16)],
        compiler_params=params(2),
        cost_estimate=cost_of(4 * length * length * part, 4 * length * (length + part)),
        name="x_transforms",
    )(cols, table, lam_x, lam_y)


def y_back(rows_in, table):
    slabs, rows, part = rows_in.shape
    width = slabs * part
    block = min(512, width)
    return pl.pallas_call(
        y_back_kernel,
        grid=(width // block,),
        out_shape=jax.ShapeDtypeStruct((rows, width), jnp.float32),
        in_specs=[
            whole((slabs, rows, part)),
            pl.BlockSpec((width, block), lambda j: (0, j)),
        ],
        out_specs=pl.BlockSpec((rows, block), lambda j: (0, j)),
        scratch_shapes=[pltpu.VMEM((rows, width), jnp.bfloat16)],
        compiler_params=params(1),
        cost_estimate=cost_of(2 * rows * width * width, 2 * width * (width + 3 * rows)),
        name="y_back",
    )(rows_in, table)


def exchange(buf):
    return lax.all_to_all(buf, "slab", split_axis=0, concat_axis=0, tiled=True)


def local(wind, obs_velocity, gate_weight, azimuth, block_owner, block_cell):
    slabs = lax.axis_size("slab")
    here = lax.axis_index("slab")
    field = wind[0]
    width_x, _, width_y = field.shape
    total_x = width_x * slabs
    part_y = width_y // slabs
    blocks, _ = obs_velocity.shape
    capacity = 2 * blocks // slabs

    owner = block_owner[:, 0]
    match = (owner[:, None] == lax.iota(jnp.int32, slabs)[None, :]).astype(jnp.int32)
    before = jnp.cumsum(match, axis=0) - match
    slot = owner * capacity + jnp.sum(before * match, axis=1)
    wc = gate_weight * jnp.cos(azimuth)
    ws = gate_weight * jnp.sin(azimuth)
    coefs = jnp.stack(
        [
            jnp.sum(wc * wc, axis=1),
            jnp.sum(wc * ws, axis=1),
            jnp.sum(ws * ws, axis=1),
            jnp.sum(wc * obs_velocity, axis=1),
            jnp.sum(ws * obs_velocity, axis=1),
            block_cell.astype(jnp.float32),
        ]
    )
    cost_own = 0.5 * jnp.sum(obs_velocity * obs_velocity)
    placed = (slot[:, None] == lax.iota(jnp.int32, slabs * capacity)[None, :]).astype(jnp.float32)
    sent = jnp.dot(coefs, placed, precision=lax.Precision.HIGHEST)
    sent = sent.reshape(6, slabs, capacity).transpose(1, 0, 2)
    got = exchange(jnp.concatenate([sent, jnp.zeros((slabs, 2, capacity), jnp.float32)], axis=1))
    cells = jnp.round(got[:, 5]).astype(jnp.int32)

    ends = slabs - 1
    low = lax.ppermute(field[width_x - 2 :], "slab", [(i, i + 1) for i in range(ends)])
    high = lax.ppermute(field[:2], "slab", [(i + 1, i) for i in range(ends)])
    pad = jnp.zeros((halo - 2, 2, width_y), jnp.float32)
    wind_ext = jnp.concatenate([pad, low, field, high, pad], axis=0).transpose(1, 0, 2)

    gradient, cost_part = gradient_of(cells, got, wind_ext, width_x, total_x)

    table_y = lax.optimization_barrier(dst_table(width_y))
    table_x = table_y if total_x == width_y else lax.optimization_barrier(dst_table(total_x))
    lam_x = eigen_values(total_x, 0, total_x)[:, None]
    lam_y = eigen_values(width_y, here * part_y, part_y)[None, :]

    spectra = [exchange(y_forward(gradient, c, table_y, slabs)) for c in range(2)]
    solved = [x_transforms(cols, table_x, lam_x, lam_y) for cols in spectra]
    energy_part = jnp.sum(solved[0][1]) + jnp.sum(solved[1][1])
    sums = lax.psum(
        jnp.stack([cost_own + cost_part[0, 0], energy_part]), ("slab", "radar")
    )
    cost_total = sums[0]
    precond = [y_back(exchange(back), table_y) for back, _ in solved]
    updated = field - cost_total / sums[1] * jnp.stack(precond, axis=1)
    return (updated[None], jnp.reshape(cost_total, (1,)))


def solution(mesh):
    return jax.shard_map(
        local,
        mesh=mesh,
        in_specs=(
            P(("groups", "radar"), "slab", None, None),
            P(("groups", "slab", "radar"), None),
            P(("groups", "slab", "radar"), None),
            P(("groups", "slab", "radar"), None),
            P(("groups", "slab", "radar"), None),
            P(("groups", "slab", "radar")),
        ),
        out_specs=(P(("groups", "radar"), "slab", None, None), P("groups")),
        check_vma=False,
    )
```

time: 696 us -> 381 us (0.55); the launches traced: 684 us -> 377 us
  other arithmetic: 259 us -> 32.8 us
  matrix products: 127 us -> 0.81 us
  local copies, waits for them, and re-layouts: 155 us -> 47.9 us
  Pallas kernels: 0 us -> 107 us
  waiting for transfers between devices: 13.4 us -> 98.7 us
  starting transfers between devices: 90 us -> 29.3 us
  blocking collectives: 35 us -> 56.3 us
    dot_general x3 -> x0, other arithmetic: 143 us -> none  [the longest x1 66.2 us: local(): jnp.dot(table_x, scaled.astype(jnp.bfloat16).reshape(total_x, 2 * part_y)...]
    dot_general x4 -> x1, matrix products: 127 us -> 0.81 us  [local(): sent = jnp.dot(coefs, placed, precision=lax.Precision.HIGHEST)]
    pallas_call x0 -> x7, Pallas kernels: none -> 107 us  [the longest x1 40.8 us: gradient_of(): pl.pallas_call(functools.partial(gradient_kernel, ends), out_shape=(jax.S...]
    all_to_all x6 -> x5, waiting for transfers between devices: 13.4 us -> 98.7 us  [exchange(): return lax.all_to_all(buf, 'slab', split_axis=0, concat_axis=0, tiled=True)]
    convert_element_type x1 -> x3, other arithmetic: 66.2 us -> 6.52 us  [the longest x1 5.83 us: dst_table(): return table.astype(jnp.bfloat16).reshape(length, length)]
    all_to_all x6 -> x5, starting transfers between devices: 79 us -> 23.9 us  [exchange(): return lax.all_to_all(buf, 'slab', split_axis=0, concat_axis=0, tiled=True)]
    all_to_all x3 -> x0, local copies, waits for them, and re-layouts: 35 us -> none  [the longest x1 19.9 us: local(): lax.all_to_all(spec_y, 'slab', split_axis=2, concat_axis=0, tiled=True)]
    gather x2 -> x0, local copies, waits for them, and re-layouts: 27.1 us -> none  [the longest x1 13.6 us: local(): flat[index_u][:, None]]
  transfers between devices with their start and end apart: 10 -> 7, of which waited for: 1 -> 3; matrix products, arithmetic and copies ran while one was open for 40% -> 12% of each run, Pallas kernels for 0% -> 13%
where the time goes in v1:
time: 381 us; the launch traced here: 377 us
  Pallas kernels  107 us (28%)
  waiting for transfers between devices  98.7 us (26%)
  blocking collectives  56.3 us (15%)
  local copies, waits for them, and re-layouts  47.9 us (13%)
  other arithmetic  32.8 us (9%)
  starting transfers between devices  29.3 us (8%)
  between operations  4.57 us (1%)
    all_to_all x5, waiting for transfers between devices, exchange(): return lax.all_to_all(buf, 'slab', split_axis=0, concat_axis=0, tiled=True)  98.7 us
    psum x1, blocking collectives, local(): lax.psum(jnp.stack([cost_own + cost_part[0, 0], energy_part]), ('slab', '...  56.3 us
    pallas_call x1, Pallas kernels, gradient_of(): pl.pallas_call(functools.partial(gradient_kernel, ends), out_shape=(jax.S...  40.8 us
    pallas_call x2, Pallas kernels, x_transforms(): pl.pallas_call(x_kernel, grid=(2, length // block), out_shape=(jax.ShapeD...  29.7 us
    unnamed x17, local copies, waits for them, and re-layouts  25.9 us
    all_to_all x5, starting transfers between devices, exchange(): return lax.all_to_all(buf, 'slab', split_axis=0, concat_axis=0, tiled=True)  23.9 us
    concatenate x1, local copies, waits for them, and re-layouts, local(): jnp.concatenate([pad, low, field, high, pad], axis=0).transpose(1, 0, 2)  20.5 us
    pallas_call x2, Pallas kernels, y_back(): pl.pallas_call(y_back_kernel, grid=(width // block,), out_shape=jax.Shape...  18.7 us
  transfers between devices with their start and end apart: 7, of which 3 were waited for; matrix products, arithmetic and copies ran while one was open for 12% of the time, Pallas kernels for 13%

profile of v1, /device:TPU:0, one launch (start us, length us, event | category | flops | bytes accessed | tf_op | source)
XLA Modules:
  0.0 377.2 jit_solution(14001116983394470127)
XLA Ops:
  9.6 6.3 %all-to-all-start = ((f32[4,8,256]{2,1,0:T(8,128)}), f32[4,8,256]{2,1,0:T(8,128)S(1)}, u32[]{:S(2)}, u32[]{:S(2)}) async-start(f32[4,8,256]{2,1,0:T(8,128)} %concatenate.13), calls=%async_computation | async-start | bytes 65536 | tf_op jit(solution)/shard_map/all_to_all | solution.py:266
  15.9 8.2 %copy.32 = f32[1,512,2,2048]{3,1,2,0:T(8,128)S(1)} copy(f32[1,512,2,2048]{3,2,1,0:T(2,128)} %param.6) | data formatting | bytes 16777216 | tf_op args[0]
  24.2 3.4 copy-done
  27.6 3.9 %collective-permute-start = (f32[2,2,2048]{2,0,1:T(2,128)S(1)}, f32[2,2,2048]{2,0,1:T(2,128)S(1)}, u32[]{:S(2)}, u32[]{:S(2)}) collective-permute-start(f32[2,2,2048]{2,0,1:T(2,128)S(1)} %get-tuple-element.35), channel_id=1, source_target_pairs={{0,4},{4,8},{8,12},{1,5},{5,9},{9,13},{2,6},{6,10},{10,14},{3,7},{... | collective-permute-start | bytes 98312 | tf_op jit(solution)/shard_map/ppermute | solution.py:303
  36.4 5.8 %add_convert_fusion = bf16[32,64,2048]{2,1,0:T(8,128)(2,1)} fusion(f32[64,2048]{1,0:T(8,128)S(1)} %get-tuple-element.17, f32[32,2048]{1,0:T(8,128)S(1)} %get-tuple-element.16, f32[64,2048]{1,0:T(8,128)S(1)} %get-tuple-element.15, f32[32,2048]{1,0:T(8,128)S(1)} %get-tuple-element.14), kind=kLoop, calls=%fused_computation | loop fusion | flops 16777216 | bytes 9961472 | tf_op jit(solution)/shard_map/convert_element_type | solution.py:34
  42.2 20.5 %concatenate.14 = f32[528,2,2048]{2,0,1:T(8,128)} concatenate(f32[6,2,2048]{2,0,1:T(8,128)S(1)} %broadcast_in_dim.2, f32[2,2,2048]{2,0,1:T(2,128)S(1)} %collective-permute-done, f32[512,2,2048]{2,0,1:T(8,128)} %bitcast.52, f32[2,2,2048]{2,0,1:T(2,128)S(1)} %collective-permute-done.1, f32[6,2,2048]{2,0,1:T(8,128)S(1)} %broadcast_in_dim.2), dimensions={0} | concatenate | bytes 17301504 | tf_op jit(solution)/shard_map/concatenate | solution.py:306
  63.3 40.8 %gradient.1 = (bf16[2,512,2048]{2,1,0:T(8,128)(2,1)}, f32[1,1]{1,0:T(1,128)}) custom-call(s32[4,256]{1,0:T(4,128)} %bitcast.64, f32[4,8,256]{2,1,0:T(8,128)} %copy-done.5, f32[2,528,2048]{2,1,0:T(8,128)} %bitcast.51), custom_call_target="tpu_custom_call" | custom-call | flops 62914560 | bytes 12582912 | tf_op jit(solution)/shard_map/gradient/pallas_call | solution.py:180
  104.1 8.7 %y_forward.2 = bf16[4,512,512]{2,1,0:T(8,128)(2,1)} custom-call(bf16[2,512,2048]{2,1,0:T(8,128)(2,1)} %get-tuple-element.13.grad_ref, bf16[2048,2048]{1,0:T(8,128)(2,1)} %bitcast.53), custom_call_target="tpu_custom_call" | custom-call | flops 4294967296 | bytes 12582912 | tf_op jit(solution)/shard_map/y_forward/pallas_call | solution.py:202
  112.9 5.7 %all-to-all-start.1 = ((bf16[4,512,512]{2,1,0:T(8,128)(2,1)}), bf16[4,512,512]{2,1,0:T(8,128)(2,1)S(1)}, u32[]{:S(2)}, u32[]{:S(2)}) async-start(bf16[4,512,512]{2,1,0:T(8,128)(2,1)} %y_forward.2), calls=%async_computation.1 | async-start | bytes 4194304 | tf_op jit(solution)/shard_map/all_to_all | solution.py:266
  118.6 8.7 %y_forward.3 = bf16[4,512,512]{2,1,0:T(8,128)(2,1)} custom-call(bf16[2,512,2048]{2,1,0:T(8,128)(2,1)} %get-tuple-element.13.grad_ref, bf16[2048,2048]{1,0:T(8,128)(2,1)} %bitcast.54), custom_call_target="tpu_custom_call" | custom-call | flops 4294967296 | bytes 12582912 | tf_op jit(solution)/shard_map/y_forward/pallas_call | solution.py:202
  127.3 38.3 %all-to-all-done.1.cols_ref = bf16[4,512,512]{2,1,0:T(8,128)(2,1)S(1)} async-done(((bf16[4,512,512]{2,1,0:T(8,128)(2,1)}), bf16[4,512,512]{2,1,0:T(8,128)(2,1)S(1)}, u32[]{:S(2)}, u32[]{:S(2)}) %all-to-all-start.1) | async-done | bytes 2097184 | tf_op jit(solution)/shard_map/all_to_all | solution.py:266
  167.0 3.6 all-to-all-start.2
  171.3 4.4 %multiply_multiply_fusion.lam_x_ref = f32[2048,1]{1,0:T(8,128)} fusion(), kind=kLoop, calls=%fused_computation.5 | loop fusion | flops 10240 | bytes 8192 | tf_op jit(solution)/shard_map/mul | solution.py:39
  175.6 14.9 %x_transforms.2 = (bf16[4,512,512]{2,1,0:T(8,128)(2,1)}, f32[8,512]{1,0:T(8,128)}) custom-call(bf16[4,512,512]{2,1,0:T(8,128)(2,1)} %copy-done.4, bf16[2048,2048]{1,0:T(8,128)(2,1)} %bitcast.55, f32[2048,1]{1,0:T(8,128)} %multiply_multiply_fusion.lam_x_ref, f32[1,512]{1,0:T(1,128)} %multiply_multiply_fusion.1.lam_y_ref), custom_call_target="tpu_custom_call" | custom-call | flops 8589934592 | bytes 20971520 | tf_op jit(solution)/shard_map/x_transforms/pallas_call | solution.py:221
  190.5 27.8 %all-to-all-done.2.cols_ref = bf16[4,512,512]{2,1,0:T(8,128)(2,1)S(1)} async-done(((bf16[4,512,512]{2,1,0:T(8,128)(2,1)}), bf16[4,512,512]{2,1,0:T(8,128)(2,1)S(1)}, u32[]{:S(2)}, u32[]{:S(2)}) %all-to-all-start.2) | async-done | bytes 2097184 | tf_op jit(solution)/shard_map/all_to_all | solution.py:266
  219.6 3.8 %all-to-all-start.3 = ((bf16[4,512,512]{2,1,0:T(8,128)(2,1)}), bf16[4,512,512]{2,1,0:T(8,128)(2,1)S(1)}, u32[]{:S(2)}, u32[]{:S(2)}) async-start(bf16[4,512,512]{2,1,0:T(8,128)(2,1)} %get-tuple-element.20), calls=%async_computation.3 | async-start | bytes 4194304 | tf_op jit(solution)/shard_map/all_to_all | solution.py:266
  223.4 14.9 %x_transforms.3 = (bf16[4,512,512]{2,1,0:T(8,128)(2,1)}, f32[8,512]{1,0:T(8,128)}) custom-call(bf16[4,512,512]{2,1,0:T(8,128)(2,1)} %copy-done.3, bf16[2048,2048]{1,0:T(8,128)(2,1)} %bitcast.56, f32[2048,1]{1,0:T(8,128)} %multiply_multiply_fusion.lam_x_ref, f32[1,512]{1,0:T(1,128)} %multiply_multiply_fusion.1.lam_y_ref), custom_call_target="tpu_custom_call" | custom-call | flops 8589934592 | bytes 20971520 | tf_op jit(solution)/shard_map/x_transforms/pallas_call | solution.py:221
  238.3 32.5 %all-to-all-done.3.rows_ref = bf16[4,512,512]{2,1,0:T(8,128)(2,1)S(1)} async-done(((bf16[4,512,512]{2,1,0:T(8,128)(2,1)}), bf16[4,512,512]{2,1,0:T(8,128)(2,1)S(1)}, u32[]{:S(2)}, u32[]{:S(2)}) %all-to-all-start.3) | async-done | bytes 2097184 | tf_op jit(solution)/shard_map/all_to_all | solution.py:266
  270.8 4.5 %all-to-all-start.4 = ((bf16[4,512,512]{2,1,0:T(8,128)(2,1)}), bf16[4,512,512]{2,1,0:T(8,128)(2,1)}, u32[]{:S(2)}, u32[]{:S(2)}) async-start(bf16[4,512,512]{2,1,0:T(8,128)(2,1)} %get-tuple-element.21), calls=%async_computation.4 | async-start | bytes 4194304 | tf_op jit(solution)/shard_map/all_to_all | solution.py:266
  279.8 56.3 %psum.7 = f32[2]{0:T(128)S(1)} all-reduce(f32[2]{0:T(128)S(1)} %pad_maximum_fusion), channel_id=1, replica_groups=mesh['groups'=2,'slab'=4,'radar'=4] {'slab','radar'}, use_global_device_ids=true, to_apply=%region_11.12 | all-reduce | flops 2 | bytes 16 | tf_op jit(solution)/shard_map/psum | solution.py:318
  338.1 9.3 %y_back.2 = f32[512,2048]{1,0:T(8,128)} custom-call(bf16[4,512,512]{2,1,0:T(8,128)(2,1)} %copy-done.2, bf16[2048,2048]{1,0:T(8,128)(2,1)} %bitcast.57), custom_call_target="tpu_custom_call" | custom-call | flops 4294967296 | bytes 14680064 | tf_op jit(solution)/shard_map/y_back/pallas_call | solution.py:249
  347.4 9.4 %y_back.3 = f32[512,2048]{1,0:T(8,128)} custom-call(bf16[4,512,512]{2,1,0:T(8,128)(2,1)} %all-to-all-done.4.rows_ref, bf16[2048,2048]{1,0:T(8,128)(2,1)} %bitcast.58), custom_call_target="tpu_custom_call" | custom-call | flops 4294967296 | bytes 14680064 | tf_op jit(solution)/shard_map/y_back/pallas_call | solution.py:249
  356.8 9.3 %fusion = f32[1,512,2,2048]{3,1,2,0:T(8,128)S(1)} fusion(f32[1,512,1,2048]{3,1,2,0:T(8,128)} %bitcast.60, f32[1,512,1,2048]{3,1,2,0:T(8,128)S(1)} %bitcast.59, f32[]{:T(128)} %bitcast.21, f32[1,512,2,2048]{3,2,1,0:T(2,128)} %param.6), kind=kLoop, calls=%fused_computation.2 | loop fusion | flops 6291456 | bytes 25165828 | tf_op jit(solution)/shard_map/sub | solution.py:323
  366.1 11.1 %copy.23 = f32[1,512,2,2048]{3,2,1,0:T(2,128)} copy(f32[1,512,2,2048]{3,1,2,0:T(8,128)S(1)} %fusion) | data formatting | bytes 16777216
  (44 shorter events, 20.3 us)
Async XLA Ops:
  9.6 53.1 %all-to-all-start = ((f32[4,8,256]{2,1,0:T(8,128)}), f32[4,8,256]{2,1,0:T(8,128)S(1)}, u32[]{:S(2)}, u32[]{:S(2)}) async-start(f32[4,8,256]{2,1,0:T(8,128)} %concatenate.13), calls=%async_computation | async-start | bytes 65536 | tf_op jit(solution)/shard_map/all_to_all | solution.py:266
  24.1 3.4 copy-start
  27.6 14.6 %collective-permute-start = (f32[2,2,2048]{2,0,1:T(2,128)S(1)}, f32[2,2,2048]{2,0,1:T(2,128)S(1)}, u32[]{:S(2)}, u32[]{:S(2)}) collective-permute-start(f32[2,2,2048]{2,0,1:T(2,128)S(1)} %get-tuple-element.35), channel_id=1, source_target_pairs={{0,4},{4,8},{8,12},{1,5},{5,9},{9,13},{2,6},{6,10},{10,14},{3,7},{... | collective-permute-start | bytes 98312 | tf_op jit(solution)/shard_map/ppermute | solution.py:303
  31.5 10.7 %collective-permute-start.1 = (f32[2,2,2048]{2,0,1:T(2,128)S(1)}, f32[2,2,2048]{2,0,1:T(2,128)S(1)}, u32[]{:S(2)}, u32[]{:S(2)}) collective-permute-start(f32[2,2,2048]{2,0,1:T(2,128)S(1)} %get-tuple-element.34), channel_id=1, source_target_pairs={{4,0},{8,4},{12,8},{5,1},{9,5},{13,9},{6,2},{10,6},{14,10},{7,3},{... | collective-permute-start | bytes 98312 | tf_op jit(solution)/shard_map/ppermute | solution.py:304
  62.7 0.6 copy-start.5
  112.9 52.8 %all-to-all-start.1 = ((bf16[4,512,512]{2,1,0:T(8,128)(2,1)}), bf16[4,512,512]{2,1,0:T(8,128)(2,1)S(1)}, u32[]{:S(2)}, u32[]{:S(2)}) async-start(bf16[4,512,512]{2,1,0:T(8,128)(2,1)} %y_forward.2), calls=%async_computation.1 | async-start | bytes 4194304 | tf_op jit(solution)/shard_map/all_to_all | solution.py:266
  165.7 1.3 copy-start.4
  167.0 51.3 %all-to-all-start.2 = ((bf16[4,512,512]{2,1,0:T(8,128)(2,1)}), bf16[4,512,512]{2,1,0:T(8,128)(2,1)S(1)}, u32[]{:S(2)}, u32[]{:S(2)}) async-start(bf16[4,512,512]{2,1,0:T(8,128)(2,1)} %y_forward.3), calls=%async_computation.2 | async-start | bytes 4194304 | tf_op jit(solution)/shard_map/all_to_all | solution.py:266
  218.2 1.3 copy-start.3
  219.6 51.3 %all-to-all-start.3 = ((bf16[4,512,512]{2,1,0:T(8,128)(2,1)}), bf16[4,512,512]{2,1,0:T(8,128)(2,1)S(1)}, u32[]{:S(2)}, u32[]{:S(2)}) async-start(bf16[4,512,512]{2,1,0:T(8,128)(2,1)} %get-tuple-element.20), calls=%async_computation.3 | async-start | bytes 4194304 | tf_op jit(solution)/shard_map/all_to_all | solution.py:266
  223.4 53.1 %copy-start.6 = (f32[8,512]{1,0:T(8,128)S(1)}, f32[8,512]{1,0:T(8,128)}, u32[]{:S(2)}) copy-start(f32[8,512]{1,0:T(8,128)} %get-tuple-element.18) | copy-start | bytes 49156
  270.8 67.2 %copy-start.2 = (bf16[4,512,512]{2,1,0:T(8,128)(2,1)}, bf16[4,512,512]{2,1,0:T(8,128)(2,1)S(1)}, u32[]{:S(2)}) copy-start(bf16[4,512,512]{2,1,0:T(8,128)(2,1)S(1)} %all-to-all-done.3.rows_ref) | copy-start | bytes 6291460
  270.8 76.5 %all-to-all-start.4 = ((bf16[4,512,512]{2,1,0:T(8,128)(2,1)}), bf16[4,512,512]{2,1,0:T(8,128)(2,1)}, u32[]{:S(2)}, u32[]{:S(2)}) async-start(bf16[4,512,512]{2,1,0:T(8,128)(2,1)} %get-tuple-element.21), calls=%async_computation.4 | async-start | bytes 4194304 | tf_op jit(solution)/shard_map/all_to_all | solution.py:266
  347.4 9.4 %copy-start.1 = (f32[512,2048]{1,0:T(8,128)S(1)}, f32[512,2048]{1,0:T(8,128)}, u32[]{:S(2)}) copy-start(f32[512,2048]{1,0:T(8,128)} %y_back.2) | copy-start | bytes 12582916

commit v2 on v1

--- a/solution.py
+++ b/solution.py
@@ -39,14 +39,18 @@
     return 4.0 * jnp.sin(math.pi / (2 * (length + 1)) * waves) ** 2
 
 
-def gradient_kernel(ends, cell_ref, coef_ref, wind_ref, out_ref, cost_ref, grad_ref, sum_ref):
-    _, rows, width = out_ref.shape
+def gradient_kernel(component, ends, cell_ref, coef_ref, wind_ref, low_ref, high_ref, *refs):
+    out_ref, grad_ref = refs[0], refs[-1]
+    rows, width = out_ref.shape
     slabs, _, capacity = coef_ref.shape
     here = lax.axis_index("slab")
     step = min(32, rows)
+    count = rows // step
     tall = step + 2 * halo
-
-    sum_ref[...] = jnp.zeros_like(sum_ref)
+    with_cost = component == 1
+    if with_cost:
+        cost_ref, sum_ref = refs[1], refs[2]
+        sum_ref[...] = jnp.zeros_like(sum_ref)
     lane = lax.broadcasted_iota(jnp.int32, (tall, width), 1)
     row = lax.broadcasted_iota(jnp.int32, (tall, width), 0)
 
@@ -57,23 +61,35 @@
 
     def stencil(i, carry):
         start = pl.multiple_of(i * step, 8)
-        u = wind_ref[0, pl.ds(start, tall), :]
-        v = wind_ref[1, pl.ds(start, tall), :]
+        above = pl.ds(pl.multiple_of(jnp.maximum(start - halo, 0), 8), halo)
+        below = pl.ds(pl.multiple_of(jnp.minimum(start + step, rows - halo), 8), halo)
+
+        def tall_block(c):
+            return jnp.concatenate(
+                [
+                    jnp.where(i == 0, low_ref[c], wind_ref[c, above, :]),
+                    wind_ref[c, pl.ds(start, step), :],
+                    jnp.where(i == count - 1, high_ref[c], wind_ref[c, below, :]),
+                ],
+                axis=0,
+            )
+
+        u, v = tall_block(0), tall_block(1)
         before, after = y_sides(v)
         div = 0.5 * (pltpu.roll(u, tall - 1, 0) - pltpu.roll(u, 1, 0)) + 0.5 * (after - before)
         place = here * rows + start - halo + row
         div = jnp.where((place >= 0) & (place < ends), div, 0.0)
-        kept = div[halo : halo + step]
-        sum_ref[...] += jnp.sum((kept * kept).reshape(step // 8, 8, width), axis=0)
-        grad_u = pltpu.roll(div, 1, 0) - pltpu.roll(div, tall - 1, 0)
-        before, after = y_sides(div)
-        grad_v = before - after
-        scale = divergence_weight * 0.5
-        grad_ref[0, pl.ds(start, step), :] = scale * grad_u[halo : halo + step]
-        grad_ref[1, pl.ds(start, step), :] = scale * grad_v[halo : halo + step]
-        return carry
-
-    lax.fori_loop(0, rows // step, stencil, 0)
+        if with_cost:
+            kept = div[halo : halo + step]
+            sum_ref[...] += jnp.sum((kept * kept).reshape(step // 8, 8, width), axis=0)
+            before, after = y_sides(div)
+            grad = before - after
+        else:
+            grad = pltpu.roll(div, 1, 0) - pltpu.roll(div, tall - 1, 0)
+        grad_ref[pl.ds(start, step), :] = divergence_weight * 0.5 * grad[halo : halo + step]
+        return carry
+
+    lax.fori_loop(0, count, stencil, 0)
 
     spot = lax.broadcasted_iota(jnp.int32, (8, 128), 0) * 128
     spot = spot + lax.broadcasted_iota(jnp.int32, (8, 128), 1)
@@ -85,15 +101,20 @@
         top = pl.multiple_of(x // 8 * 8, 8)
         first = pl.multiple_of(y // 128 * 128, 128)
         mask = spot == (x - top) * 128 + (y - first)
-        u = wind_ref[0, pl.ds(pl.multiple_of(top + halo, 8), 8), pl.ds(first, 128)]
-        v = wind_ref[1, pl.ds(pl.multiple_of(top + halo, 8), 8), pl.ds(first, 128)]
-        uu, uv, vv = coef_ref[s, 0, i], coef_ref[s, 1, i], coef_ref[s, 2, i]
-        ou, ov = coef_ref[s, 3, i], coef_ref[s, 4, i]
-        part_u = uu * u + uv * v - ou
-        part_v = uv * u + vv * v - ov
-        grad_ref[0, pl.ds(top, 8), pl.ds(first, 128)] += jnp.where(mask, part_u, 0.0)
-        grad_ref[1, pl.ds(top, 8), pl.ds(first, 128)] += jnp.where(mask, part_v, 0.0)
-        return total + jnp.where(mask, u * (part_u - ou) + v * (part_v - ov), 0.0)
+        u = wind_ref[0, pl.ds(top, 8), pl.ds(first, 128)]
+        v = wind_ref[1, pl.ds(top, 8), pl.ds(first, 128)]
+        uv = coef_ref[s, 1, i]
+        if with_cost:
+            uu, vv = coef_ref[s, 0, i], coef_ref[s, 2, i]
+            ou, ov = coef_ref[s, 3, i], coef_ref[s, 4, i]
+            part = uv * u + vv * v - ov
+            total = total + jnp.where(
+                mask, u * (uu * u + uv * v - 2.0 * ou) + v * (part - ov), 0.0
+            )
+        else:
+            part = coef_ref[s, 0, i] * u + uv * v - coef_ref[s, 3, i]
+        grad_ref[pl.ds(top, 8), pl.ds(first, 128)] += jnp.where(mask, part, 0.0)
+        return total
 
     def gate_group(t, total):
         s = t // (capacity // 8)
@@ -105,21 +126,21 @@
     total = lax.fori_loop(
         0, slabs * capacity // 8, gate_group, jnp.zeros((8, 128), jnp.float32)
     )
-    cost_div = 0.5 * divergence_weight * jnp.sum(sum_ref[...], keepdims=True)
-    cost_ref[...] = cost_div + 0.5 * jnp.sum(total, keepdims=True)
+    if with_cost:
+        cost_div = 0.5 * divergence_weight * jnp.sum(sum_ref[...], keepdims=True)
+        cost_ref[...] = cost_div + 0.5 * jnp.sum(total, keepdims=True)
 
     def lower(i, carry):
         at = pl.ds(pl.multiple_of(i * step, 16), step)
-        out_ref[0, at, :] = grad_ref[0, at, :].astype(jnp.bfloat16)
-        out_ref[1, at, :] = grad_ref[1, at, :].astype(jnp.bfloat16)
-        return carry
-
-    lax.fori_loop(0, rows // step, lower, 0)
+        out_ref[at, :] = grad_ref[at, :].astype(jnp.bfloat16)
+        return carry
+
+    lax.fori_loop(0, count, lower, 0)
 
 
 def y_forward_kernel(grad_ref, table_ref, out_ref):
     parts, _, part = out_ref.shape
-    spec = jnp.dot(grad_ref[0], table_ref[...], preferred_element_type=jnp.float32)
+    spec = jnp.dot(grad_ref[...], table_ref[...], preferred_element_type=jnp.float32)
     spec = spec.astype(jnp.bfloat16)
     for d in range(parts):
         out_ref[d] = spec[:, d * part : (d + 1) * part]
@@ -173,30 +194,29 @@
     )
 
 
-def gradient_of(cells, coefs, wind_ext, rows, ends):
-    _, tall, width = wind_ext.shape
+def gradient_of(component, cells, coefs, field, low, high, ends):
+    _, rows, width = field.shape
     smem = pl.BlockSpec(memory_space=pltpu.SMEM)
     vmem = pl.BlockSpec(memory_space=pltpu.VMEM)
-    return pl.pallas_call(
-        functools.partial(gradient_kernel, ends),
-        out_shape=(
-            jax.ShapeDtypeStruct((2, rows, width), jnp.bfloat16),
-            jax.ShapeDtypeStruct((1, 1), jnp.float32),
-        ),
-        in_specs=[smem, smem, vmem],
-        out_specs=(vmem, vmem),
-        scratch_shapes=[
-            pltpu.VMEM((2, rows, width), jnp.float32),
-            pltpu.VMEM((8, width), jnp.float32),
-        ],
+    out_shape = [jax.ShapeDtypeStruct((rows, width), jnp.bfloat16)]
+    scratch = [pltpu.VMEM((rows, width), jnp.float32)]
+    if component == 1:
+        out_shape.append(jax.ShapeDtypeStruct((1, 1), jnp.float32))
+        scratch.insert(0, pltpu.VMEM((8, width), jnp.float32))
+    return pl.pallas_call(
+        functools.partial(gradient_kernel, component, ends),
+        out_shape=out_shape,
+        in_specs=[smem, smem, vmem, vmem, vmem],
+        out_specs=[vmem] * len(out_shape),
+        scratch_shapes=scratch,
         compiler_params=pltpu.CompilerParams(vmem_limit_bytes=vmem_bytes),
         cost_estimate=cost_of(60 * rows * width, 12 * rows * width),
-        name="gradient",
-    )(cells, coefs, wind_ext)
-
-
-def y_forward(grad, component, table, slabs):
-    _, rows, width = grad.shape
+        name="gradient_" + "uv"[component],
+    )(cells, coefs, field, low, high)
+
+
+def y_forward(grad, table, slabs):
+    rows, width = grad.shape
     part = width // slabs
     block = max(part, min(512, width))
     return pl.pallas_call(
@@ -204,7 +224,7 @@
         grid=(width // block,),
         out_shape=jax.ShapeDtypeStruct((slabs, rows, part), jnp.bfloat16),
         in_specs=[
-            pl.BlockSpec((1, rows, width), lambda j: (component, 0, 0)),
+            whole((rows, width)),
             pl.BlockSpec((width, block), lambda j: (0, j)),
         ],
         out_specs=pl.BlockSpec((block // part, rows, part), lambda j: (j, 0, 0)),
@@ -260,6 +280,116 @@
         cost_estimate=cost_of(2 * rows * width * width, 2 * width * (width + 3 * rows)),
         name="y_back",
     )(rows_in, table)
+
+
+def last_kernel(step_ref, rows_ref, table_ref, other_ref, wind_ref, out_ref, held_ref, pre_ref):
+    slabs, rows, part = rows_ref.shape
+    step = step_ref[0]
+    some = min(32, rows)
+
+    @pl.when(pl.program_id(0) == 0)
+    def _():
+        for d in range(slabs):
+            held_ref[:, d * part : (d + 1) * part] = rows_ref[d]
+
+    pre_ref[...] = jnp.dot(held_ref[...], table_ref[...], preferred_element_type=jnp.float32)
+
+    def update(i, carry):
+        at = pl.ds(pl.multiple_of(i * some, some), some)
+        out_ref[at, 0, :] = wind_ref[at, 0, :] - step * other_ref[at, :]
+        out_ref[at, 1, :] = wind_ref[at, 1, :] - step * pre_ref[at, :]
+        return carry
+
+    lax.fori_loop(0, rows // some, update, 0)
+
+
+def last(step, rows_in, table, other, field):
+    slabs, rows, part = rows_in.shape
+    width = slabs * part
+    block = min(512, width)
+    return pl.pallas_call(
+        last_kernel,
+        grid=(width // block,),
+        out_shape=jax.ShapeDtypeStruct((rows, 2, width), jnp.float32),
+        in_specs=[
+            pl.BlockSpec(memory_space=pltpu.SMEM),
+            whole((slabs, rows, part)),
+            pl.BlockSpec((width, block), lambda j: (0, j)),
+            pl.BlockSpec((rows, block), lambda j: (0, j)),
+            pl.BlockSpec((rows, 2, block), lambda j: (0, 0, j)),
+        ],
+        out_specs=pl.BlockSpec((rows, 2, block), lambda j: (0, 0, j)),
+        scratch_shapes=[
+            pltpu.VMEM((rows, width), jnp.bfloat16),
+            pltpu.VMEM((rows, block), jnp.float32),
+        ],
+        compiler_params=params(1),
+        cost_estimate=cost_of(2 * rows * width * width, 2 * width * (width + 11 * rows)),
+        name="last",
+    )(step, rows_in, table, other, field)
+
+
+def sum_kernel(radars, own_ref, out_ref, slots, send_sem, recv_sem):
+    count = slots.shape[0]
+    me = lax.axis_index("slab") * radars + lax.axis_index("radar")
+
+    def peer(k):
+        other = lax.rem(me + k, count)
+        return {"slab": other // radars, "radar": lax.rem(other, radars)}
+
+    def came(k):
+        return lax.rem(me + count - k, count)
+
+    def copy(k, slot):
+        return pltpu.make_async_remote_copy(
+            src_ref=own_ref,
+            dst_ref=slots.at[slot],
+            send_sem=send_sem.at[k],
+            recv_sem=recv_sem.at[slot],
+            device_id=peer(k),
+            device_id_type=pl.DeviceIdType.MESH,
+        )
+
+    barrier = pltpu.get_barrier_semaphore()
+
+    def greet(k, carry):
+        pl.semaphore_signal(
+            barrier, inc=1, device_id=peer(k), device_id_type=pl.DeviceIdType.MESH
+        )
+        return carry
+
+    def send(k, carry):
+        copy(k, me).start()
+        return carry
+
+    def finish(k, carry):
+        copy(k, me).wait_send()
+        copy(k, came(k)).wait_recv()
+        return carry
+
+    lax.fori_loop(1, count, greet, 0)
+    pl.semaphore_wait(barrier, count - 1)
+    lax.fori_loop(1, count, send, 0)
+    slots[me] = own_ref[...]
+    lax.fori_loop(1, count, finish, 0)
+    out_ref[...] = jnp.sum(slots[...], axis=0)
+
+
+def summed(own, slabs, radars):
+    count = slabs * radars
+    return pl.pallas_call(
+        functools.partial(sum_kernel, radars),
+        out_shape=jax.ShapeDtypeStruct(own.shape, jnp.float32),
+        in_specs=[pl.BlockSpec(memory_space=pltpu.VMEM)],
+        out_specs=pl.BlockSpec(memory_space=pltpu.VMEM),
+        scratch_shapes=[
+            pltpu.VMEM((count,) + own.shape, jnp.float32),
+            pltpu.SemaphoreType.DMA((count,)),
+            pltpu.SemaphoreType.DMA((count,)),
+        ],
+        compiler_params=pltpu.CompilerParams(collective_id=0, has_side_effects=True),
+        name="summed",
+    )(own)
 
 
 def exchange(buf):
@@ -303,24 +433,27 @@
     low = lax.ppermute(field[width_x - 2 :], "slab", [(i, i + 1) for i in range(ends)])
     high = lax.ppermute(field[:2], "slab", [(i + 1, i) for i in range(ends)])
     pad = jnp.zeros((halo - 2, 2, width_y), jnp.float32)
-    wind_ext = jnp.concatenate([pad, low, field, high, pad], axis=0).transpose(1, 0, 2)
-
-    gradient, cost_part = gradient_of(cells, got, wind_ext, width_x, total_x)
-
+    low = jnp.concatenate([pad, low], axis=0).transpose(1, 0, 2)
+    high = jnp.concatenate([high, pad], axis=0).transpose(1, 0, 2)
+    apart = lax.optimization_barrier(field.transpose(1, 0, 2))
+    grad_u = gradient_of(0, cells, got, apart, low, high, total_x)[0]
     table_y = lax.optimization_barrier(dst_table(width_y))
     table_x = table_y if total_x == width_y else lax.optimization_barrier(dst_table(total_x))
     lam_x = eigen_values(total_x, 0, total_x)[:, None]
     lam_y = eigen_values(width_y, here * part_y, part_y)[None, :]
 
-    spectra = [exchange(y_forward(gradient, c, table_y, slabs)) for c in range(2)]
+    spec_u, cells_v = lax.optimization_barrier((y_forward(grad_u, table_y, slabs), cells))
+    grad_v, cost_part = gradient_of(1, cells_v, got, apart, low, high, total_x)
+    spectra = [exchange(spec_u), exchange(y_forward(grad_v, table_y, slabs))]
     solved = [x_transforms(cols, table_x, lam_x, lam_y) for cols in spectra]
     energy_part = jnp.sum(solved[0][1]) + jnp.sum(solved[1][1])
-    sums = lax.psum(
-        jnp.stack([cost_own + cost_part[0, 0], energy_part]), ("slab", "radar")
-    )
-    cost_total = sums[0]
-    precond = [y_back(exchange(back), table_y) for back, _ in solved]
-    updated = field - cost_total / sums[1] * jnp.stack(precond, axis=1)
+    lane = lax.broadcasted_iota(jnp.int32, (8, 128), 1)
+    own = jnp.where(lane == 0, cost_own + cost_part[0, 0], energy_part)
+    sums = summed(own, slabs, lax.axis_size("radar"))
+    cost_total = sums[0, 0]
+    step = jnp.reshape(cost_total / sums[0, 1], (1,))
+    rows_u, rows_v = exchange(solved[0][0]), exchange(solved[1][0])
+    updated = last(step, rows_v, table_y, y_back(rows_u, table_y), field)
     return (updated[None], jnp.reshape(cost_total, (1,)))
 
 

time: 381 us -> 327 us (0.86)
  Pallas kernels: 107 us -> 188 us
  blocking collectives: 56.3 us -> 0 us
  waiting for transfers between devices: 98.7 us -> 62.2 us
  local copies, waits for them, and re-layouts: 47.9 us -> 16.7 us
  other arithmetic: 32.8 us -> 23.4 us
    pallas_call x1 -> x4, Pallas kernels: 40.8 us -> 132 us  [the longest x2 71 us: gradient_of(): pl.pallas_call(functools.partial(gradient_kernel, component, ends), out_s...]
    psum x1 -> x0, blocking collectives: 56.3 us -> none  [local(): lax.psum(jnp.stack([cost_own + cost_part[0, 0], energy_part]), ('slab', '...]
    all_to_all x5, waiting for transfers between devices: 98.7 us -> 62.2 us  [exchange(): return lax.all_to_all(buf, 'slab', split_axis=0, concat_axis=0, tiled=True)]
    unnamed x17 -> x15, local copies, waits for them, and re-layouts: 25.9 us -> 3.4 us
    concatenate x1 -> x0, local copies, waits for them, and re-layouts: 20.5 us -> none  [local(): jnp.concatenate([pad, low, field, high, pad], axis=0).transpose(1, 0, 2)]
    pallas_call x2 -> x1, Pallas kernels: 18.7 us -> 9.37 us  [y_back(): pl.pallas_call(y_back_kernel, grid=(width // block,), out_shape=jax.Shape...]
    sub x1 -> x0, other arithmetic: 9.34 us -> none  [local(): updated = field - cost_total / sums[1] * jnp.stack(precond, axis=1)]
    optimization_barrier x0 -> x1, local copies, waits for them, and re-layouts: none -> 8.25 us  [local(): apart = lax.optimization_barrier(field.transpose(1, 0, 2))]
  transfers between devices with their start and end apart: 7 -> 7, of which waited for: 3 -> 3; matrix products, arithmetic and copies ran while one was open for 12% -> 9% of each run, Pallas kernels for 13% -> 40%
where the time goes in v2:
time: 327 us; the launch traced here: 325 us
  Pallas kernels  188 us (57%)
  waiting for transfers between devices  62.2 us (19%)
  starting transfers between devices  29.2 us (9%)
  other arithmetic  23.4 us (7%)
  local copies, waits for them, and re-layouts  16.7 us (5%)
  between operations  4.59 us (1%)
    pallas_call x2, Pallas kernels, gradient_of(): pl.pallas_call(functools.partial(gradient_kernel, component, ends), out_s...  71 us
    all_to_all x5, waiting for transfers between devices, exchange(): return lax.all_to_all(buf, 'slab', split_axis=0, concat_axis=0, tiled=True)  62.2 us
    pallas_call x1, Pallas kernels, summed(): pl.pallas_call(functools.partial(sum_kernel, radars), out_shape=jax.Shape...  45.5 us
    pallas_call x2, Pallas kernels, x_transforms(): pl.pallas_call(x_kernel, grid=(2, length // block), out_shape=(jax.ShapeD...  29.7 us
    all_to_all x5, starting transfers between devices, exchange(): return lax.all_to_all(buf, 'slab', split_axis=0, concat_axis=0, tiled=True)  23.7 us
    pallas_call x2, Pallas kernels, y_forward(): pl.pallas_call(y_forward_kernel, grid=(width // block,), out_shape=jax.Sh...  17.4 us
    pallas_call x1, Pallas kernels, last(): pl.pallas_call(last_kernel, grid=(width // block,), out_shape=jax.ShapeDt...  15.3 us
    pallas_call x1, Pallas kernels, y_back(): pl.pallas_call(y_back_kernel, grid=(width // block,), out_shape=jax.Shape...  9.37 us
  transfers between devices with their start and end apart: 7, of which 3 were waited for; matrix products, arithmetic and copies ran while one was open for 9% of the time, Pallas kernels for 40%

profile of v2, /device:TPU:0, one launch (start us, length us, event | category | flops | bytes accessed | tf_op | source)
XLA Modules:
  0.0 325.3 jit_solution(549937242742402865)
XLA Ops:
  5.1 3.0 multiply_reduce_fusion
  9.6 6.3 %all-to-all-start = ((f32[4,8,256]{2,1,0:T(8,128)}), f32[4,8,256]{2,1,0:T(8,128)S(1)}, u32[]{:S(2)}, u32[]{:S(2)}) async-start(f32[4,8,256]{2,1,0:T(8,128)} %concatenate.9), calls=%async_computation | async-start | bytes 65536 | tf_op jit(solution)/shard_map/all_to_all | solution.py:396
  16.9 4.2 %collective-permute-start = (f32[2,2,2048]{2,0,1:T(2,128)S(1)}, f32[2,2,2048]{2,0,1:T(2,128)S(1)}, u32[]{:S(2)}, u32[]{:S(2)}) collective-permute-start(f32[2,2,2048]{2,0,1:T(2,128)S(1)} %bitcast.65), channel_id=1, source_target_pairs={{0,4},{4,8},{8,12},{1,5},{5,9},{9,13},{2,6},{6,10},{10,14},{3,7},{... | collective-permute-start | bytes 98312 | tf_op jit(solution)/shard_map/ppermute | solution.py:433
  23.6 2.2 fusion.6
  25.8 5.8 %add_convert_fusion = bf16[32,64,2048]{2,1,0:T(8,128)(2,1)} fusion(f32[64,2048]{1,0:T(8,128)S(1)} %get-tuple-element.17, f32[32,2048]{1,0:T(8,128)S(1)} %get-tuple-element.16, f32[64,2048]{1,0:T(8,128)S(1)} %get-tuple-element.15, f32[32,2048]{1,0:T(8,128)S(1)} %get-tuple-element.14), kind=kLoop, calls=%fused_computation | loop fusion | flops 16777216 | bytes 9961472 | tf_op jit(solution)/shard_map/convert_element_type | solution.py:34
  31.6 8.3 %copy.18.wind_ref = f32[2,512,2048]{2,1,0:T(8,128)} copy(f32[2,512,2048]{2,0,1:T(2,128)S(1)} %bitcast.55) | data formatting | bytes 16777216 | tf_op jit(solution)/shard_map/optimization_barrier | solution.py:438
  41.8 34.2 %gradient_u.1.grad_ref = bf16[512,2048]{1,0:T(8,128)(2,1)} custom-call(s32[4,256]{1,0:T(4,128)} %bitcast.63, f32[4,8,256]{2,1,0:T(8,128)} %copy-done.4, f32[2,512,2048]{2,1,0:T(8,128)} %copy.18.wind_ref, f32[2,8,2048]{2,1,0:T(8,128)} %pad_bitcast_fusion.1.low_ref, f32[2,8,2048]{2,1,0:T(8,128)} %pad_bitcast_fusion.high_ref), custom_call_target="tpu_custom_call" | custom-call | flops 62914560 | bytes 12582912 | tf_op jit(solution)/shard_map/gradient_u/pallas_call | solution.py:206
  76.0 8.7 %y_forward.2 = bf16[4,512,512]{2,1,0:T(8,128)(2,1)} custom-call(bf16[512,2048]{1,0:T(8,128)(2,1)} %gradient_u.1.grad_ref, bf16[2048,2048]{1,0:T(8,128)(2,1)} %bitcast.56), custom_call_target="tpu_custom_call" | custom-call | flops 4294967296 | bytes 12582912 | tf_op jit(solution)/shard_map/y_forward/pallas_call | solution.py:222
  84.7 5.7 %all-to-all-start.1 = ((bf16[4,512,512]{2,1,0:T(8,128)(2,1)}), bf16[4,512,512]{2,1,0:T(8,128)(2,1)S(1)}, u32[]{:S(2)}, u32[]{:S(2)}) async-start(bf16[4,512,512]{2,1,0:T(8,128)(2,1)} %y_forward.2), calls=%async_computation.1 | async-start | bytes 4194304 | tf_op jit(solution)/shard_map/all_to_all | solution.py:396
  90.4 36.8 %gradient_v.1 = (bf16[512,2048]{1,0:T(8,128)(2,1)}, f32[1,1]{1,0:T(1,128)}) custom-call(s32[4,256]{1,0:T(4,128)} %bitcast.64, f32[4,8,256]{2,1,0:T(8,128)} %copy-done.4, f32[2,512,2048]{2,1,0:T(8,128)} %copy.18.wind_ref, f32[2,8,2048]{2,1,0:T(8,128)} %pad_bitcast_fusion.1.low_ref, f32[2,8,2048]{2,1,0:T(8,128)} %pad_bitcast_fusion.high_ref), custom_call_target="tpu_custom_call" | custom-call | flops 62914560 | bytes 12582912 | tf_op jit(solution)/shard_map/gradient_v/pallas_call | solution.py:206
  127.2 8.7 %y_forward.3 = bf16[4,512,512]{2,1,0:T(8,128)(2,1)} custom-call(bf16[512,2048]{1,0:T(8,128)(2,1)} %get-tuple-element.22.grad_ref, bf16[2048,2048]{1,0:T(8,128)(2,1)} %bitcast.57), custom_call_target="tpu_custom_call" | custom-call | flops 4294967296 | bytes 12582912 | tf_op jit(solution)/shard_map/y_forward/pallas_call | solution.py:222
  136.0 1.5 all-to-all-done.1.cols_ref
  137.5 4.5 %all-to-all-start.2 = ((bf16[4,512,512]{2,1,0:T(8,128)(2,1)}), bf16[4,512,512]{2,1,0:T(8,128)(2,1)}, u32[]{:S(2)}, u32[]{:S(2)}) async-start(bf16[4,512,512]{2,1,0:T(8,128)(2,1)} %y_forward.3), calls=%async_computation.2 | async-start | bytes 4194304 | tf_op jit(solution)/shard_map/all_to_all | solution.py:396
  142.6 4.4 %multiply_multiply_fusion.lam_x_ref = f32[2048,1]{1,0:T(8,128)} fusion(), kind=kLoop, calls=%fused_computation.3 | loop fusion | flops 10240 | bytes 8192 | tf_op jit(solution)/shard_map/mul | solution.py:39
  147.0 14.9 %x_transforms.2 = (bf16[4,512,512]{2,1,0:T(8,128)(2,1)}, f32[8,512]{1,0:T(8,128)}) custom-call(bf16[4,512,512]{2,1,0:T(8,128)(2,1)} %copy-done.3, bf16[2048,2048]{1,0:T(8,128)(2,1)} %bitcast.58, f32[2048,1]{1,0:T(8,128)} %multiply_multiply_fusion.lam_x_ref, f32[1,512]{1,0:T(1,128)} %multiply_multiply_fusion.1.lam_y_ref), custom_call_target="tpu_custom_call" | custom-call | flops 8589934592 | bytes 20971520 | tf_op jit(solution)/shard_map/x_transforms/pallas_call | solution.py:241
  161.9 27.9 %all-to-all-done.2.cols_ref = bf16[4,512,512]{2,1,0:T(8,128)(2,1)} async-done(((bf16[4,512,512]{2,1,0:T(8,128)(2,1)}), bf16[4,512,512]{2,1,0:T(8,128)(2,1)}, u32[]{:S(2)}, u32[]{:S(2)}) %all-to-all-start.2) | async-done | bytes 2097184 | tf_op jit(solution)/shard_map/all_to_all | solution.py:396
  189.7 3.6 %all-to-all-start.4 = ((bf16[4,512,512]{2,1,0:T(8,128)(2,1)}), bf16[4,512,512]{2,1,0:T(8,128)(2,1)S(1)}, u32[]{:S(2)}, u32[]{:S(2)}) async-start(bf16[4,512,512]{2,1,0:T(8,128)(2,1)} %get-tuple-element.25), calls=%async_computation.4 | async-start | bytes 4194304 | tf_op jit(solution)/shard_map/all_to_all | solution.py:396
  193.3 14.9 %x_transforms.3 = (bf16[4,512,512]{2,1,0:T(8,128)(2,1)}, f32[8,512]{1,0:T(8,128)}) custom-call(bf16[4,512,512]{2,1,0:T(8,128)(2,1)} %all-to-all-done.2.cols_ref, bf16[2048,2048]{1,0:T(8,128)(2,1)} %bitcast.59, f32[2048,1]{1,0:T(8,128)} %multiply_multiply_fusion.lam_x_ref, f32[1,512]{1,0:T(1,128)} %multiply_multiply_fusion.1.lam_y_ref), custom_call_target="tpu_custom_call" | custom-call | flops 8589934592 | bytes 20971520 | tf_op jit(solution)/shard_map/x_transforms/pallas_call | solution.py:241
  208.2 32.8 %all-to-all-done.4.rows_ref = bf16[4,512,512]{2,1,0:T(8,128)(2,1)S(1)} async-done(((bf16[4,512,512]{2,1,0:T(8,128)(2,1)}), bf16[4,512,512]{2,1,0:T(8,128)(2,1)S(1)}, u32[]{:S(2)}, u32[]{:S(2)}) %all-to-all-start.4) | async-done | bytes 2097184 | tf_op jit(solution)/shard_map/all_to_all | solution.py:396
  242.3 3.6 %all-to-all-start.3 = ((bf16[4,512,512]{2,1,0:T(8,128)(2,1)}), bf16[4,512,512]{2,1,0:T(8,128)(2,1)S(1)}, u32[]{:S(2)}, u32[]{:S(2)}) async-start(bf16[4,512,512]{2,1,0:T(8,128)(2,1)} %get-tuple-element.24), calls=%async_computation.3 | async-start | bytes 4194304 | tf_op jit(solution)/shard_map/all_to_all | solution.py:396
  247.2 1.4 reduce_sum.92
  251.1 45.5 %summed.1 = f32[8,128]{1,0:T(8,128)} custom-call(f32[8,128]{1,0:T(8,128)} %iota.59.own_ref), custom_call_target="tpu_custom_call" | custom-call | tf_op jit(solution)/shard_map/summed/pallas_call | solution.py:380
  299.3 9.4 %y_back.1.other_ref = f32[512,2048]{1,0:T(8,128)} custom-call(bf16[4,512,512]{2,1,0:T(8,128)(2,1)} %copy-done.2, bf16[2048,2048]{1,0:T(8,128)(2,1)} %bitcast.60), custom_call_target="tpu_custom_call" | custom-call | flops 4294967296 | bytes 14680064 | tf_op jit(solution)/shard_map/y_back/pallas_call | solution.py:269
  310.0 15.3 %last.1 = f32[512,2,2048]{2,1,0:T(2,128)} custom-call(f32[1]{0:T(128)} %bitcast.21.step_ref, bf16[4,512,512]{2,1,0:T(8,128)(2,1)} %copy-done.1, bf16[2048,2048]{1,0:T(8,128)(2,1)} %bitcast.61, f32[512,2048]{1,0:T(8,128)} %y_back.1.other_ref, f32[512,2,2048]{2,1,0:T(2,128)} %bitcast.54), custom_call_target="tpu_custom_call" | custom-call | flops 4294967296 | bytes 31457280 | tf_op jit(solution)/shard_map/last/pallas_call | solution.py:310
  (44 shorter events, 17.2 us)
Async XLA Ops:
  9.6 31.6 %all-to-all-start = ((f32[4,8,256]{2,1,0:T(8,128)}), f32[4,8,256]{2,1,0:T(8,128)S(1)}, u32[]{:S(2)}, u32[]{:S(2)}) async-start(f32[4,8,256]{2,1,0:T(8,128)} %concatenate.9), calls=%async_computation | async-start | bytes 65536 | tf_op jit(solution)/shard_map/all_to_all | solution.py:396
  15.9 15.7 %copy-start = (f32[1,512,2,2048]{3,2,1,0:T(2,128)S(1)}, f32[1,512,2,2048]{3,2,1,0:T(2,128)}, u32[]{:S(2)}) copy-start(f32[1,512,2,2048]{3,2,1,0:T(2,128)} %param.6) | copy-start | bytes 25165828
  16.9 23.6 %collective-permute-start = (f32[2,2,2048]{2,0,1:T(2,128)S(1)}, f32[2,2,2048]{2,0,1:T(2,128)S(1)}, u32[]{:S(2)}, u32[]{:S(2)}) collective-permute-start(f32[2,2,2048]{2,0,1:T(2,128)S(1)} %bitcast.65), channel_id=1, source_target_pairs={{0,4},{4,8},{8,12},{1,5},{5,9},{9,13},{2,6},{6,10},{10,14},{3,7},{... | collective-permute-start | bytes 98312 | tf_op jit(solution)/shard_map/ppermute | solution.py:433
  21.1 18.7 %collective-permute-start.1 = (f32[2,2,2048]{2,0,1:T(2,128)S(1)}, f32[2,2,2048]{2,0,1:T(2,128)S(1)}, u32[]{:S(2)}, u32[]{:S(2)}) collective-permute-start(f32[2,2,2048]{2,0,1:T(2,128)S(1)} %bitcast.66), channel_id=1, source_target_pairs={{4,0},{8,4},{12,8},{5,1},{9,5},{13,9},{6,2},{10,6},{14,10},{7,3},{... | collective-permute-start | bytes 98312 | tf_op jit(solution)/shard_map/ppermute | solution.py:434
  41.2 0.6 copy-start.4
  84.7 52.8 %all-to-all-start.1 = ((bf16[4,512,512]{2,1,0:T(8,128)(2,1)}), bf16[4,512,512]{2,1,0:T(8,128)(2,1)S(1)}, u32[]{:S(2)}, u32[]{:S(2)}) async-start(bf16[4,512,512]{2,1,0:T(8,128)(2,1)} %y_forward.2), calls=%async_computation.1 | async-start | bytes 4194304 | tf_op jit(solution)/shard_map/all_to_all | solution.py:396
  137.5 9.5 %copy-start.3 = (bf16[4,512,512]{2,1,0:T(8,128)(2,1)}, bf16[4,512,512]{2,1,0:T(8,128)(2,1)S(1)}, u32[]{:S(2)}) copy-start(bf16[4,512,512]{2,1,0:T(8,128)(2,1)S(1)} %all-to-all-done.1.cols_ref) | copy-start | bytes 6291460
  137.5 52.3 %all-to-all-start.2 = ((bf16[4,512,512]{2,1,0:T(8,128)(2,1)}), bf16[4,512,512]{2,1,0:T(8,128)(2,1)}, u32[]{:S(2)}, u32[]{:S(2)}) async-start(bf16[4,512,512]{2,1,0:T(8,128)(2,1)} %y_forward.3), calls=%async_computation.2 | async-start | bytes 4194304 | tf_op jit(solution)/shard_map/all_to_all | solution.py:396
  189.7 51.3 %all-to-all-start.4 = ((bf16[4,512,512]{2,1,0:T(8,128)(2,1)}), bf16[4,512,512]{2,1,0:T(8,128)(2,1)S(1)}, u32[]{:S(2)}, u32[]{:S(2)}) async-start(bf16[4,512,512]{2,1,0:T(8,128)(2,1)} %get-tuple-element.25), calls=%async_computation.4 | async-start | bytes 4194304 | tf_op jit(solution)/shard_map/all_to_all | solution.py:396
  193.3 55.2 %copy-start.5 = (f32[8,512]{1,0:T(8,128)S(1)}, f32[8,512]{1,0:T(8,128)}, u32[]{:S(2)}) copy-start(f32[8,512]{1,0:T(8,128)} %get-tuple-element.21) | copy-start | bytes 49156
  241.0 1.4 copy-start.2
  242.3 66.3 %all-to-all-start.3 = ((bf16[4,512,512]{2,1,0:T(8,128)(2,1)}), bf16[4,512,512]{2,1,0:T(8,128)(2,1)S(1)}, u32[]{:S(2)}, u32[]{:S(2)}) async-start(bf16[4,512,512]{2,1,0:T(8,128)(2,1)} %get-tuple-element.24), calls=%async_computation.3 | async-start | bytes 4194304 | tf_op jit(solution)/shard_map/all_to_all | solution.py:396
  308.6 1.4 copy-start.1

commit v3 on v2

--- a/solution.py
+++ b/solution.py
@@ -40,7 +40,7 @@
 
 
 def gradient_kernel(component, ends, cell_ref, coef_ref, wind_ref, low_ref, high_ref, *refs):
-    out_ref, grad_ref = refs[0], refs[-1]
+    out_ref, grad_ref, apart_ref = refs[0], refs[-2], refs[-1]
     rows, width = out_ref.shape
     slabs, _, capacity = coef_ref.shape
     here = lax.axis_index("slab")
@@ -65,11 +65,13 @@
         below = pl.ds(pl.multiple_of(jnp.minimum(start + step, rows - halo), 8), halo)
 
         def tall_block(c):
+            middle = wind_ref[pl.ds(start, step), c, :]
+            apart_ref[c, pl.ds(start, step), :] = middle
             return jnp.concatenate(
                 [
-                    jnp.where(i == 0, low_ref[c], wind_ref[c, above, :]),
-                    wind_ref[c, pl.ds(start, step), :],
-                    jnp.where(i == count - 1, high_ref[c], wind_ref[c, below, :]),
+                    jnp.where(i == 0, low_ref[c], wind_ref[above, c, :]),
+                    middle,
+                    jnp.where(i == count - 1, high_ref[c], wind_ref[below, c, :]),
                 ],
                 axis=0,
             )
@@ -95,14 +97,11 @@
     spot = spot + lax.broadcasted_iota(jnp.int32, (8, 128), 1)
 
     def gate_block(s, i, total):
-        cell = cell_ref[s, i]
-        x = cell // width
-        y = cell - x * width
-        top = pl.multiple_of(x // 8 * 8, 8)
-        first = pl.multiple_of(y // 128 * 128, 128)
-        mask = spot == (x - top) * 128 + (y - first)
-        u = wind_ref[0, pl.ds(top, 8), pl.ds(first, 128)]
-        v = wind_ref[1, pl.ds(top, 8), pl.ds(first, 128)]
+        top = pl.multiple_of(cell_ref[s, 0, i], 8)
+        first = pl.multiple_of(cell_ref[s, 1, i], 128)
+        mask = spot == cell_ref[s, 2, i]
+        u = apart_ref[0, pl.ds(top, 8), pl.ds(first, 128)]
+        v = apart_ref[1, pl.ds(top, 8), pl.ds(first, 128)]
         uv = coef_ref[s, 1, i]
         if with_cost:
             uu, vv = coef_ref[s, 0, i], coef_ref[s, 2, i]
@@ -116,16 +115,15 @@
         grad_ref[pl.ds(top, 8), pl.ds(first, 128)] += jnp.where(mask, part, 0.0)
         return total
 
-    def gate_group(t, total):
-        s = t // (capacity // 8)
-        base = (t - s * (capacity // 8)) * 8
+    def gate_group(s, t, total):
         for k in range(8):
-            total = gate_block(s, base + k, total)
+            total = gate_block(s, t * 8 + k, total)
         return total
 
-    total = lax.fori_loop(
-        0, slabs * capacity // 8, gate_group, jnp.zeros((8, 128), jnp.float32)
-    )
+    def gate_slab(s, total):
+        return lax.fori_loop(0, capacity // 8, functools.partial(gate_group, s), total)
+
+    total = lax.fori_loop(0, slabs, gate_slab, jnp.zeros((8, 128), jnp.float32))
     if with_cost:
         cost_div = 0.5 * divergence_weight * jnp.sum(sum_ref[...], keepdims=True)
         cost_ref[...] = cost_div + 0.5 * jnp.sum(total, keepdims=True)
@@ -195,11 +193,14 @@
 
 
 def gradient_of(component, cells, coefs, field, low, high, ends):
-    _, rows, width = field.shape
+    rows, _, width = field.shape
     smem = pl.BlockSpec(memory_space=pltpu.SMEM)
     vmem = pl.BlockSpec(memory_space=pltpu.VMEM)
     out_shape = [jax.ShapeDtypeStruct((rows, width), jnp.bfloat16)]
-    scratch = [pltpu.VMEM((rows, width), jnp.float32)]
+    scratch = [
+        pltpu.VMEM((rows, width), jnp.float32),
+        pltpu.VMEM((2, rows, width), jnp.float32),
+    ]
     if component == 1:
         out_shape.append(jax.ShapeDtypeStruct((1, 1), jnp.float32))
         scratch.insert(0, pltpu.VMEM((8, width), jnp.float32))
@@ -428,6 +429,8 @@
     sent = sent.reshape(6, slabs, capacity).transpose(1, 0, 2)
     got = exchange(jnp.concatenate([sent, jnp.zeros((slabs, 2, capacity), jnp.float32)], axis=1))
     cells = jnp.round(got[:, 5]).astype(jnp.int32)
+    x, y = cells // width_y, cells % width_y
+    cells = jnp.stack([x // 8 * 8, y // 128 * 128, x % 8 * 128 + y % 128], axis=1)
 
     ends = slabs - 1
     low = lax.ppermute(field[width_x - 2 :], "slab", [(i, i + 1) for i in range(ends)])
@@ -435,24 +438,25 @@
     pad = jnp.zeros((halo - 2, 2, width_y), jnp.float32)
     low = jnp.concatenate([pad, low], axis=0).transpose(1, 0, 2)
     high = jnp.concatenate([high, pad], axis=0).transpose(1, 0, 2)
-    apart = lax.optimization_barrier(field.transpose(1, 0, 2))
-    grad_u = gradient_of(0, cells, got, apart, low, high, total_x)[0]
+    grad_u = gradient_of(0, cells, got, field, low, high, total_x)[0]
     table_y = lax.optimization_barrier(dst_table(width_y))
     table_x = table_y if total_x == width_y else lax.optimization_barrier(dst_table(total_x))
     lam_x = eigen_values(total_x, 0, total_x)[:, None]
     lam_y = eigen_values(width_y, here * part_y, part_y)[None, :]
 
     spec_u, cells_v = lax.optimization_barrier((y_forward(grad_u, table_y, slabs), cells))
-    grad_v, cost_part = gradient_of(1, cells_v, got, apart, low, high, total_x)
+    grad_v, cost_part = gradient_of(1, cells_v, got, field, low, high, total_x)
     spectra = [exchange(spec_u), exchange(y_forward(grad_v, table_y, slabs))]
     solved = [x_transforms(cols, table_x, lam_x, lam_y) for cols in spectra]
     energy_part = jnp.sum(solved[0][1]) + jnp.sum(solved[1][1])
     lane = lax.broadcasted_iota(jnp.int32, (8, 128), 1)
     own = jnp.where(lane == 0, cost_own + cost_part[0, 0], energy_part)
+    rows_u, own = lax.optimization_barrier((exchange(solved[0][0]), own))
     sums = summed(own, slabs, lax.axis_size("radar"))
     cost_total = sums[0, 0]
     step = jnp.reshape(cost_total / sums[0, 1], (1,))
-    rows_u, rows_v = exchange(solved[0][0]), exchange(solved[1][0])
+    back_v, step = lax.optimization_barrier((solved[1][0], step))
+    rows_v = exchange(back_v)
     updated = last(step, rows_v, table_y, y_back(rows_u, table_y), field)
     return (updated[None], jnp.reshape(cost_total, (1,)))
 

time: 327 us -> 302 us (0.924)
  Pallas kernels: 188 us -> 123 us
  waiting for transfers between devices: 62.2 us -> 111 us
  local copies, waits for them, and re-layouts: 16.7 us -> 9.02 us
    all_to_all x5, waiting for transfers between devices: 62.2 us -> 111 us  [exchange(): return lax.all_to_all(buf, 'slab', split_axis=0, concat_axis=0, tiled=True)]
    pallas_call x1, Pallas kernels: 45.5 us -> 8.03 us  [summed(): pl.pallas_call(functools.partial(sum_kernel, radars), out_shape=jax.Shape...]
    pallas_call x2, Pallas kernels: 71 us -> 42.8 us  [gradient_of(): pl.pallas_call(functools.partial(gradient_kernel, component, ends), out_s...]
    optimization_barrier x1 -> x0, local copies, waits for them, and re-layouts: 8.25 us -> none  [local(): apart = lax.optimization_barrier(field.transpose(1, 0, 2))]
  transfers between devices with their start and end apart: 7 -> 7, of which waited for: 3 -> 4; matrix products, arithmetic and copies ran while one was open for 9% -> 6% of each run, Pallas kernels for 40% -> 23%
where the time goes in v3:
time: 302 us; the launch traced here: 301 us
  Pallas kernels  123 us (41%)
  waiting for transfers between devices  111 us (37%)
  starting transfers between devices  28.4 us (9%)
  other arithmetic  24.1 us (8%)
  local copies, waits for them, and re-layouts  9.02 us (3%)
  between operations  4.73 us (2%)
    all_to_all x5, waiting for transfers between devices, exchange(): return lax.all_to_all(buf, 'slab', split_axis=0, concat_axis=0, tiled=True)  111 us
    pallas_call x2, Pallas kernels, gradient_of(): pl.pallas_call(functools.partial(gradient_kernel, component, ends), out_s...  42.8 us
    pallas_call x2, Pallas kernels, x_transforms(): pl.pallas_call(x_kernel, grid=(2, length // block), out_shape=(jax.ShapeD...  29.7 us
    all_to_all x5, starting transfers between devices, exchange(): return lax.all_to_all(buf, 'slab', split_axis=0, concat_axis=0, tiled=True)  23.1 us
    pallas_call x2, Pallas kernels, y_forward(): pl.pallas_call(y_forward_kernel, grid=(width // block,), out_shape=jax.Sh...  17.4 us
    pallas_call x1, Pallas kernels, last(): pl.pallas_call(last_kernel, grid=(width // block,), out_shape=jax.ShapeDt...  15.3 us
    pallas_call x1, Pallas kernels, y_back(): pl.pallas_call(y_back_kernel, grid=(width // block,), out_shape=jax.Shape...  9.37 us
    pallas_call x1, Pallas kernels, summed(): pl.pallas_call(functools.partial(sum_kernel, radars), out_shape=jax.Shape...  8.03 us
  transfers between devices with their start and end apart: 7, of which 4 were waited for; matrix products, arithmetic and copies ran while one was open for 6% of the time, Pallas kernels for 23%

profile of v3, /device:TPU:0, one launch (start us, length us, event | category | flops | bytes accessed | tf_op | source)
XLA Modules:
  0.0 300.6 jit_solution(10460109737504702880)
XLA Ops:
  5.1 3.0 %multiply_reduce_fusion.1 = (f32[512]{0:T(512)S(1)}, f32[512]{0:T(512)S(1)}, f32[512]{0:T(512)S(1)}, f32[512]{0:T(512)S(1)}, f32[512]{0:T(512)S(1)}, /*index=5*/f32[]{:T(128)}) fusion(f32[512,128]{1,0:T(8,128)} %param.7, f32[512,128]{1,0:T(8,128)} %param.8, f32[512,128]{1,0:T(8,128)} %param.9), kind=kLoop, calls=%fused_computation.23 | loop fusion | flops 914943 | bytes 796676 | tf_op jit(solution)/shard_map/reduce_sum | solution.py:422
  9.6 6.3 %all-to-all-start = ((f32[4,8,256]{2,1,0:T(8,128)}), f32[4,8,256]{2,1,0:T(8,128)S(1)}, u32[]{:S(2)}, u32[]{:S(2)}) async-start(f32[4,8,256]{2,1,0:T(8,128)} %concatenate.9), calls=%async_computation | async-start | bytes 65536 | tf_op jit(solution)/shard_map/all_to_all | solution.py:397
  16.7 3.9 %collective-permute-start = (f32[2,2,2048]{2,0,1:T(2,128)S(1)}, f32[2,2,2048]{2,0,1:T(2,128)S(1)}, u32[]{:S(2)}, u32[]{:S(2)}) collective-permute-start(f32[2,2,2048]{2,0,1:T(2,128)S(1)} %bitcast.59), channel_id=1, source_target_pairs={{0,4},{4,8},{8,12},{1,5},{5,9},{9,13},{2,6},{6,10},{10,14},{3,7},{... | collective-permute-start | bytes 98312 | tf_op jit(solution)/shard_map/ppermute | solution.py:436
  23.2 2.2 fusion.6
  25.4 5.8 %add_convert_fusion = bf16[32,64,2048]{2,1,0:T(8,128)(2,1)} fusion(f32[64,2048]{1,0:T(8,128)S(1)} %get-tuple-element.21, f32[32,2048]{1,0:T(8,128)S(1)} %get-tuple-element.20, f32[64,2048]{1,0:T(8,128)S(1)} %get-tuple-element.19, f32[32,2048]{1,0:T(8,128)S(1)} %get-tuple-element.18), kind=kLoop, calls=%fused_computation | loop fusion | flops 16777216 | bytes 9961472 | tf_op jit(solution)/shard_map/convert_element_type | solution.py:34
  33.3 20.2 %gradient_u.1.grad_ref = bf16[512,2048]{1,0:T(8,128)(2,1)} custom-call(s32[4,3,256]{2,1,0:T(4,128)} %pad_add_fusion.cell_ref, f32[4,8,256]{2,1,0:T(8,128)} %copy-done.4, f32[512,2,2048]{2,1,0:T(2,128)} %bitcast.49, f32[2,8,2048]{2,1,0:T(8,128)} %pad_bitcast_fusion.1.low_ref, f32[2,8,2048]{2,1,0:T(8,128)} %pad_bitcast_fusion.high_ref), custom_call_target="tpu_custom_call" | custom-call | flops 62914560 | bytes 12582912 | tf_op jit(solution)/shard_map/gradient_u/pallas_call | solution.py:207
  53.5 8.7 %y_forward.2 = bf16[4,512,512]{2,1,0:T(8,128)(2,1)} custom-call(bf16[512,2048]{1,0:T(8,128)(2,1)} %gradient_u.1.grad_ref, bf16[2048,2048]{1,0:T(8,128)(2,1)} %bitcast.52), custom_call_target="tpu_custom_call" | custom-call | flops 4294967296 | bytes 12582912 | tf_op jit(solution)/shard_map/y_forward/pallas_call | solution.py:223
  62.2 5.8 %all-to-all-start.2 = ((bf16[4,512,512]{2,1,0:T(8,128)(2,1)}), bf16[4,512,512]{2,1,0:T(8,128)(2,1)S(1)}, u32[]{:S(2)}, u32[]{:S(2)}) async-start(bf16[4,512,512]{2,1,0:T(8,128)(2,1)} %y_forward.2), calls=%async_computation.2 | async-start | bytes 4194304 | tf_op jit(solution)/shard_map/all_to_all | solution.py:397
  68.0 22.6 %gradient_v.1 = (bf16[512,2048]{1,0:T(8,128)(2,1)}, f32[1,1]{1,0:T(1,128)}) custom-call(s32[4,3,256]{2,1,0:T(4,128)} %pad_add_fusion.cell_ref, f32[4,8,256]{2,1,0:T(8,128)} %copy-done.4, f32[512,2,2048]{2,1,0:T(2,128)} %bitcast.50, f32[2,8,2048]{2,1,0:T(8,128)} %pad_bitcast_fusion.1.low_ref, f32[2,8,2048]{2,1,0:T(8,128)} %pad_bitcast_fusion.high_ref), custom_call_target="tpu_custom_call" | custom-call | flops 62914560 | bytes 12582912 | tf_op jit(solution)/shard_map/gradient_v/pallas_call | solution.py:207
  90.6 8.7 %y_forward.3 = bf16[4,512,512]{2,1,0:T(8,128)(2,1)} custom-call(bf16[512,2048]{1,0:T(8,128)(2,1)} %get-tuple-element.23.grad_ref, bf16[2048,2048]{1,0:T(8,128)(2,1)} %bitcast.53), custom_call_target="tpu_custom_call" | custom-call | flops 4294967296 | bytes 12582912 | tf_op jit(solution)/shard_map/y_forward/pallas_call | solution.py:223
  99.3 15.7 %all-to-all-done.2.cols_ref = bf16[4,512,512]{2,1,0:T(8,128)(2,1)S(1)} async-done(((bf16[4,512,512]{2,1,0:T(8,128)(2,1)}), bf16[4,512,512]{2,1,0:T(8,128)(2,1)S(1)}, u32[]{:S(2)}, u32[]{:S(2)}) %all-to-all-start.2) | async-done | bytes 2097184 | tf_op jit(solution)/shard_map/all_to_all | solution.py:397
  116.4 3.8 %all-to-all-start.1 = ((bf16[4,512,512]{2,1,0:T(8,128)(2,1)}), bf16[4,512,512]{2,1,0:T(8,128)(2,1)S(1)}, u32[]{:S(2)}, u32[]{:S(2)}) async-start(bf16[4,512,512]{2,1,0:T(8,128)(2,1)} %y_forward.3), calls=%async_computation.1 | async-start | bytes 4194304 | tf_op jit(solution)/shard_map/all_to_all | solution.py:397
  120.8 4.4 %multiply_multiply_fusion.lam_x_ref = f32[2048,1]{1,0:T(8,128)} fusion(), kind=kLoop, calls=%fused_computation.3 | loop fusion | flops 10240 | bytes 8192 | tf_op jit(solution)/shard_map/mul | solution.py:39
  125.2 14.8 %x_transforms.3 = (bf16[4,512,512]{2,1,0:T(8,128)(2,1)}, f32[8,512]{1,0:T(8,128)}) custom-call(bf16[4,512,512]{2,1,0:T(8,128)(2,1)} %copy-done.3, bf16[2048,2048]{1,0:T(8,128)(2,1)} %bitcast.54, f32[2048,1]{1,0:T(8,128)} %multiply_multiply_fusion.lam_x_ref, f32[1,512]{1,0:T(1,128)} %multiply_multiply_fusion.1.lam_y_ref), custom_call_target="tpu_custom_call" | custom-call | flops 8589934592 | bytes 20971520 | tf_op jit(solution)/shard_map/x_transforms/pallas_call | solution.py:242
  140.0 27.6 %all-to-all-done.1.cols_ref = bf16[4,512,512]{2,1,0:T(8,128)(2,1)S(1)} async-done(((bf16[4,512,512]{2,1,0:T(8,128)(2,1)}), bf16[4,512,512]{2,1,0:T(8,128)(2,1)S(1)}, u32[]{:S(2)}, u32[]{:S(2)}) %all-to-all-start.1) | async-done | bytes 2097184 | tf_op jit(solution)/shard_map/all_to_all | solution.py:397
  169.0 3.6 %all-to-all-start.3 = ((bf16[4,512,512]{2,1,0:T(8,128)(2,1)}), bf16[4,512,512]{2,1,0:T(8,128)(2,1)S(1)}, u32[]{:S(2)}, u32[]{:S(2)}) async-start(bf16[4,512,512]{2,1,0:T(8,128)(2,1)} %get-tuple-element.26), calls=%async_computation.3 | async-start | bytes 4194304 | tf_op jit(solution)/shard_map/all_to_all | solution.py:397
  174.5 14.9 %x_transforms.2 = (bf16[4,512,512]{2,1,0:T(8,128)(2,1)}, f32[8,512]{1,0:T(8,128)}) custom-call(bf16[4,512,512]{2,1,0:T(8,128)(2,1)} %copy-done.2, bf16[2048,2048]{1,0:T(8,128)(2,1)} %bitcast.55, f32[2048,1]{1,0:T(8,128)} %multiply_multiply_fusion.lam_x_ref, f32[1,512]{1,0:T(1,128)} %multiply_multiply_fusion.1.lam_y_ref), custom_call_target="tpu_custom_call" | custom-call | flops 8589934592 | bytes 20971520 | tf_op jit(solution)/shard_map/x_transforms/pallas_call | solution.py:242
  192.0 28.2 %all-to-all-done.3.rows_ref = bf16[4,512,512]{2,1,0:T(8,128)(2,1)S(1)} async-done(((bf16[4,512,512]{2,1,0:T(8,128)(2,1)}), bf16[4,512,512]{2,1,0:T(8,128)(2,1)S(1)}, u32[]{:S(2)}, u32[]{:S(2)}) %all-to-all-start.3) | async-done | bytes 2097184 | tf_op jit(solution)/shard_map/all_to_all | solution.py:397
  220.9 8.0 %summed.1 = f32[8,128]{1,0:T(8,128)} custom-call(f32[8,128]{1,0:T(8,128)} %iota.59.own_ref), custom_call_target="tpu_custom_call" | custom-call | tf_op jit(solution)/shard_map/summed/pallas_call | solution.py:381
  231.6 3.6 %all-to-all-start.4 = ((bf16[4,512,512]{2,1,0:T(8,128)(2,1)}), bf16[4,512,512]{2,1,0:T(8,128)(2,1)S(1)}, u32[]{:S(2)}, u32[]{:S(2)}) async-start(bf16[4,512,512]{2,1,0:T(8,128)(2,1)} %get-tuple-element.32), calls=%async_computation.4 | async-start | bytes 4194304 | tf_op jit(solution)/shard_map/all_to_all | solution.py:397
  235.2 9.4 %y_back.1.other_ref = f32[512,2048]{1,0:T(8,128)} custom-call(bf16[4,512,512]{2,1,0:T(8,128)(2,1)} %copy-done.1, bf16[2048,2048]{1,0:T(8,128)(2,1)} %bitcast.56), custom_call_target="tpu_custom_call" | custom-call | flops 4294967296 | bytes 14680064 | tf_op jit(solution)/shard_map/y_back/pallas_call | solution.py:270
  244.6 39.3 %all-to-all-done.4.rows_ref = bf16[4,512,512]{2,1,0:T(8,128)(2,1)S(1)} async-done(((bf16[4,512,512]{2,1,0:T(8,128)(2,1)}), bf16[4,512,512]{2,1,0:T(8,128)(2,1)S(1)}, u32[]{:S(2)}, u32[]{:S(2)}) %all-to-all-start.4) | async-done | bytes 2097184 | tf_op jit(solution)/shard_map/all_to_all | solution.py:397
  283.9 1.4 copy-done
  285.3 15.3 %last.1 = f32[512,2,2048]{2,1,0:T(2,128)} custom-call(f32[1]{0:T(128)} %bitcast.20.step_ref, bf16[4,512,512]{2,1,0:T(8,128)(2,1)} %copy-done, bf16[2048,2048]{1,0:T(8,128)(2,1)} %bitcast.57, f32[512,2048]{1,0:T(8,128)} %y_back.1.other_ref, f32[512,2,2048]{2,1,0:T(2,128)} %bitcast.51), custom_call_target="tpu_custom_call" | custom-call | flops 4294967296 | bytes 31457280 | tf_op jit(solution)/shard_map/last/pallas_call | solution.py:311
  (45 shorter events, 18.4 us)
Async XLA Ops:
  9.6 22.9 %all-to-all-start = ((f32[4,8,256]{2,1,0:T(8,128)}), f32[4,8,256]{2,1,0:T(8,128)S(1)}, u32[]{:S(2)}, u32[]{:S(2)}) async-start(f32[4,8,256]{2,1,0:T(8,128)} %concatenate.9), calls=%async_computation | async-start | bytes 65536 | tf_op jit(solution)/shard_map/all_to_all | solution.py:397
  16.7 15.1 %collective-permute-start = (f32[2,2,2048]{2,0,1:T(2,128)S(1)}, f32[2,2,2048]{2,0,1:T(2,128)S(1)}, u32[]{:S(2)}, u32[]{:S(2)}) collective-permute-start(f32[2,2,2048]{2,0,1:T(2,128)S(1)} %bitcast.59), channel_id=1, source_target_pairs={{0,4},{4,8},{8,12},{1,5},{5,9},{9,13},{2,6},{6,10},{10,14},{3,7},{... | collective-permute-start | bytes 98312 | tf_op jit(solution)/shard_map/ppermute | solution.py:436
  20.7 10.5 %collective-permute-start.1 = (f32[2,2,2048]{2,0,1:T(2,128)S(1)}, f32[2,2,2048]{2,0,1:T(2,128)S(1)}, u32[]{:S(2)}, u32[]{:S(2)}) collective-permute-start(f32[2,2,2048]{2,0,1:T(2,128)S(1)} %bitcast.60), channel_id=1, source_target_pairs={{4,0},{8,4},{12,8},{5,1},{9,5},{13,9},{6,2},{10,6},{14,10},{7,3},{... | collective-permute-start | bytes 98312 | tf_op jit(solution)/shard_map/ppermute | solution.py:437
  32.5 0.7 copy-start.4
  62.2 52.9 %all-to-all-start.2 = ((bf16[4,512,512]{2,1,0:T(8,128)(2,1)}), bf16[4,512,512]{2,1,0:T(8,128)(2,1)S(1)}, u32[]{:S(2)}, u32[]{:S(2)}) async-start(bf16[4,512,512]{2,1,0:T(8,128)(2,1)} %y_forward.2), calls=%async_computation.2 | async-start | bytes 4194304 | tf_op jit(solution)/shard_map/all_to_all | solution.py:397
  115.1 1.3 copy-start.3
  116.4 51.3 %all-to-all-start.1 = ((bf16[4,512,512]{2,1,0:T(8,128)(2,1)}), bf16[4,512,512]{2,1,0:T(8,128)(2,1)S(1)}, u32[]{:S(2)}, u32[]{:S(2)}) async-start(bf16[4,512,512]{2,1,0:T(8,128)(2,1)} %y_forward.3), calls=%async_computation.1 | async-start | bytes 4194304 | tf_op jit(solution)/shard_map/all_to_all | solution.py:397
  140.0 33.9 %copy-start.5 = (f32[8,512]{1,0:T(8,128)S(1)}, f32[8,512]{1,0:T(8,128)}, u32[]{:S(2)}) copy-start(f32[8,512]{1,0:T(8,128)} %get-tuple-element.28) | copy-start | bytes 49156
  167.7 1.3 copy-start.2
  169.0 51.3 %all-to-all-start.3 = ((bf16[4,512,512]{2,1,0:T(8,128)(2,1)}), bf16[4,512,512]{2,1,0:T(8,128)(2,1)S(1)}, u32[]{:S(2)}, u32[]{:S(2)}) async-start(bf16[4,512,512]{2,1,0:T(8,128)(2,1)} %get-tuple-element.26), calls=%async_computation.3 | async-start | bytes 4194304 | tf_op jit(solution)/shard_map/all_to_all | solution.py:397
  220.2 11.3 %copy-start.1 = (bf16[4,512,512]{2,1,0:T(8,128)(2,1)}, bf16[4,512,512]{2,1,0:T(8,128)(2,1)S(1)}, u32[]{:S(2)}) copy-start(bf16[4,512,512]{2,1,0:T(8,128)(2,1)S(1)} %all-to-all-done.3.rows_ref) | copy-start | bytes 6291460
  231.6 52.3 %all-to-all-start.4 = ((bf16[4,512,512]{2,1,0:T(8,128)(2,1)}), bf16[4,512,512]{2,1,0:T(8,128)(2,1)S(1)}, u32[]{:S(2)}, u32[]{:S(2)}) async-start(bf16[4,512,512]{2,1,0:T(8,128)(2,1)} %get-tuple-element.32), calls=%async_computation.4 | async-start | bytes 4194304 | tf_op jit(solution)/shard_map/all_to_all | solution.py:397
  283.9 1.4 copy-start

commit v4 on v3

--- a/solution.py
+++ b/solution.py
@@ -14,7 +14,7 @@
 halo = 8
 
 
-def dst_table(length):
+def dst_factors(length):
     inner = math.gcd(length, 64)
     outer = length // inner
     waves = lax.iota(jnp.int32, length) + 1
@@ -30,6 +30,11 @@
     coarse_s, coarse_c, fine_s, fine_c = lax.optimization_barrier(
         (scale * jnp.sin(coarse), scale * jnp.cos(coarse), jnp.sin(fine), jnp.cos(fine))
     )
+    return coarse_s, coarse_c, fine_s, fine_c
+
+
+def dst_table(length):
+    coarse_s, coarse_c, fine_s, fine_c = dst_factors(length)
     table = coarse_s[:, None, :] * fine_c[None] + coarse_c[:, None, :] * fine_s[None]
     return table.astype(jnp.bfloat16).reshape(length, length)
 
@@ -214,6 +219,38 @@
         cost_estimate=cost_of(60 * rows * width, 12 * rows * width),
         name="gradient_" + "uv"[component],
     )(cells, coefs, field, low, high)
+
+
+def y_first_kernel(grad_ref, cs_ref, cc_ref, fs_ref, fc_ref, out_ref, table_ref):
+    inner = fs_ref.shape[0]
+    for a in range(cs_ref.shape[0]):
+        rows = cs_ref[a : a + 1] * fc_ref[...] + cc_ref[a : a + 1] * fs_ref[...]
+        table_ref[a * inner : (a + 1) * inner, :] = rows.astype(jnp.bfloat16)
+    y_forward_kernel(grad_ref, table_ref, out_ref)
+
+
+def y_first(grad, slabs):
+    rows, width = grad.shape
+    part = width // slabs
+    block = max(part, min(512, width))
+    factors = dst_factors(width)
+    return pl.pallas_call(
+        y_first_kernel,
+        grid=(width // block,),
+        out_shape=(
+            jax.ShapeDtypeStruct((slabs, rows, part), jnp.bfloat16),
+            jax.ShapeDtypeStruct((width, width), jnp.bfloat16),
+        ),
+        in_specs=[whole((rows, width))]
+        + [pl.BlockSpec((f.shape[0], block), lambda j: (0, j)) for f in factors],
+        out_specs=(
+            pl.BlockSpec((block // part, rows, part), lambda j: (j, 0, 0)),
+            pl.BlockSpec((width, block), lambda j: (0, j)),
+        ),
+        compiler_params=params(1),
+        cost_estimate=cost_of(2 * rows * width * width, 2 * width * (width + 2 * rows)),
+        name="y_first",
+    )(grad, *factors)
 
 
 def y_forward(grad, table, slabs):
@@ -439,25 +476,26 @@
     low = jnp.concatenate([pad, low], axis=0).transpose(1, 0, 2)
     high = jnp.concatenate([high, pad], axis=0).transpose(1, 0, 2)
     grad_u = gradient_of(0, cells, got, field, low, high, total_x)[0]
-    table_y = lax.optimization_barrier(dst_table(width_y))
+    spec_u, table_y = y_first(grad_u, slabs)
     table_x = table_y if total_x == width_y else lax.optimization_barrier(dst_table(total_x))
     lam_x = eigen_values(total_x, 0, total_x)[:, None]
     lam_y = eigen_values(width_y, here * part_y, part_y)[None, :]
 
-    spec_u, cells_v = lax.optimization_barrier((y_forward(grad_u, table_y, slabs), cells))
+    spec_u, cells_v = lax.optimization_barrier((spec_u, cells))
     grad_v, cost_part = gradient_of(1, cells_v, got, field, low, high, total_x)
-    spectra = [exchange(spec_u), exchange(y_forward(grad_v, table_y, slabs))]
+    spec_v = y_forward(grad_v, table_y, slabs)
+    cols_u, _ = lax.optimization_barrier((exchange(spec_u), spec_v))
+    spectra = [cols_u, exchange(spec_v)]
     solved = [x_transforms(cols, table_x, lam_x, lam_y) for cols in spectra]
     energy_part = jnp.sum(solved[0][1]) + jnp.sum(solved[1][1])
     lane = lax.broadcasted_iota(jnp.int32, (8, 128), 1)
     own = jnp.where(lane == 0, cost_own + cost_part[0, 0], energy_part)
-    rows_u, own = lax.optimization_barrier((exchange(solved[0][0]), own))
+    pre_u, own = lax.optimization_barrier((y_back(exchange(solved[0][0]), table_y), own))
+    rows_v = exchange(solved[1][0])
     sums = summed(own, slabs, lax.axis_size("radar"))
     cost_total = sums[0, 0]
     step = jnp.reshape(cost_total / sums[0, 1], (1,))
-    back_v, step = lax.optimization_barrier((solved[1][0], step))
-    rows_v = exchange(back_v)
-    updated = last(step, rows_v, table_y, y_back(rows_u, table_y), field)
+    updated = last(step, rows_v, table_y, pre_u, field)
     return (updated[None], jnp.reshape(cost_total, (1,)))
 
 

time: 302 us -> 292 us (0.967)
  waiting for transfers between devices: 111 us -> 76.5 us
  Pallas kernels: 123 us -> 152 us
  other arithmetic: 24.1 us -> 19.4 us
    all_to_all x5, waiting for transfers between devices: 111 us -> 76.5 us  [exchange(): return lax.all_to_all(buf, 'slab', split_axis=0, concat_axis=0, tiled=True)]
    pallas_call x1, Pallas kernels: 8.03 us -> 37 us  [summed(): pl.pallas_call(functools.partial(sum_kernel, radars), out_shape=jax.Shape...]
    pallas_call x2 -> x1, Pallas kernels: 17.4 us -> 8.71 us  [y_forward(): pl.pallas_call(y_forward_kernel, grid=(width // block,), out_shape=jax.Sh...]
    pallas_call x0 -> x1, Pallas kernels: none -> 8.54 us  [y_first(): pl.pallas_call(y_first_kernel, grid=(width // block,), out_shape=(jax.Sha...]
    convert_element_type x1 -> x0, other arithmetic: 5.81 us -> none  [dst_table(): return table.astype(jnp.bfloat16).reshape(length, length)]
  transfers between devices with their start and end apart: 7 -> 7, of which waited for: 4 -> 3; matrix products, arithmetic and copies ran while one was open for 6% -> 5% of each run, Pallas kernels for 23% -> 37%
where the time goes in v4:
time: 292 us; the launch traced here: 291 us
  Pallas kernels  152 us (52%)
  waiting for transfers between devices  76.5 us (26%)
  starting transfers between devices  28.9 us (10%)
  other arithmetic  19.4 us (7%)
  local copies, waits for them, and re-layouts  9.05 us (3%)
  between operations  4.63 us (2%)
    all_to_all x5, waiting for transfers between devices, exchange(): return lax.all_to_all(buf, 'slab', split_axis=0, concat_axis=0, tiled=True)  76.5 us
    pallas_call x2, Pallas kernels, gradient_of(): pl.pallas_call(functools.partial(gradient_kernel, component, ends), out_s...  42.9 us
    pallas_call x1, Pallas kernels, summed(): pl.pallas_call(functools.partial(sum_kernel, radars), out_shape=jax.Shape...  37 us
    pallas_call x2, Pallas kernels, x_transforms(): pl.pallas_call(x_kernel, grid=(2, length // block), out_shape=(jax.ShapeD...  29.7 us
    all_to_all x5, starting transfers between devices, exchange(): return lax.all_to_all(buf, 'slab', split_axis=0, concat_axis=0, tiled=True)  23.7 us
    pallas_call x1, Pallas kernels, last(): pl.pallas_call(last_kernel, grid=(width // block,), out_shape=jax.ShapeDt...  15.3 us
    pallas_call x1, Pallas kernels, y_back(): pl.pallas_call(y_back_kernel, grid=(width // block,), out_shape=jax.Shape...  9.37 us
    pallas_call x1, Pallas kernels, y_forward(): pl.pallas_call(y_forward_kernel, grid=(width // block,), out_shape=jax.Sh...  8.71 us
  transfers between devices with their start and end apart: 7, of which 3 were waited for; matrix products, arithmetic and copies ran while one was open for 5% of the time, Pallas kernels for 37%

profile of v4, /device:TPU:0, one launch (start us, length us, event | category | flops | bytes accessed | tf_op | source)
XLA Modules:
  0.0 290.8 jit_solution(10146375452934226249)
XLA Ops:
  5.1 3.0 %multiply_reduce_fusion.1 = (f32[512]{0:T(512)S(1)}, f32[512]{0:T(512)S(1)}, f32[512]{0:T(512)S(1)}, f32[512]{0:T(512)S(1)}, f32[512]{0:T(512)S(1)}, /*index=5*/f32[]{:T(128)}) fusion(f32[512,128]{1,0:T(8,128)} %param.7, f32[512,128]{1,0:T(8,128)} %param.8, f32[512,128]{1,0:T(8,128)} %param.9), kind=kLoop, calls=%fused_computation.22 | loop fusion | flops 914943 | bytes 796676 | tf_op jit(solution)/shard_map/reduce_sum | solution.py:459
  9.6 6.3 %all-to-all-start = ((f32[4,8,256]{2,1,0:T(8,128)}), f32[4,8,256]{2,1,0:T(8,128)S(1)}, u32[]{:S(2)}, u32[]{:S(2)}) async-start(f32[4,8,256]{2,1,0:T(8,128)} %concatenate.9), calls=%async_computation | async-start | bytes 65536 | tf_op jit(solution)/shard_map/all_to_all | solution.py:434
  16.7 3.9 %collective-permute-start = (f32[2,2,2048]{2,0,1:T(2,128)S(1)}, f32[2,2,2048]{2,0,1:T(2,128)S(1)}, u32[]{:S(2)}, u32[]{:S(2)}) collective-permute-start(f32[2,2,2048]{2,0,1:T(2,128)S(1)} %bitcast.52), channel_id=1, source_target_pairs={{0,4},{4,8},{8,12},{1,5},{5,9},{9,13},{2,6},{6,10},{10,14},{3,7},{... | collective-permute-start | bytes 98312 | tf_op jit(solution)/shard_map/ppermute | solution.py:473
  22.0 3.3 %fusion.6 = (f32[64,2048]{1,0:T(8,128)}, f32[64,2048]{1,0:T(8,128)}) fusion(s32[2048]{0:T(1024)S(1)} %iota_add_fusion, s32[64]{0:T(128)S(1)} %iota_add_fusion.1), kind=kLoop, calls=%fused_computation.10 | loop fusion | flops 1179648 | bytes 1057024 | tf_op jit(solution)/shard_map/cos | solution.py:31
  25.3 1.9 cosine_multiply_fusion
  29.3 20.3 %gradient_u.1.grad_ref = bf16[512,2048]{1,0:T(8,128)(2,1)} custom-call(s32[4,3,256]{2,1,0:T(4,128)} %pad_add_fusion.cell_ref, f32[4,8,256]{2,1,0:T(8,128)} %copy-done.3, f32[512,2,2048]{2,1,0:T(2,128)} %bitcast.48, f32[2,8,2048]{2,1,0:T(8,128)} %pad_bitcast_fusion.1.low_ref, f32[2,8,2048]{2,1,0:T(8,128)} %pad_bitcast_fusion.high_ref), custom_call_target="tpu_custom_call" | custom-call | flops 62914560 | bytes 12582912 | tf_op jit(solution)/shard_map/gradient_u/pallas_call | solution.py:212
  49.6 8.5 %y_first.1 = (bf16[4,512,512]{2,1,0:T(8,128)(2,1)}, bf16[2048,2048]{1,0:T(8,128)(2,1)}) custom-call(bf16[512,2048]{1,0:T(8,128)(2,1)} %gradient_u.1.grad_ref, f32[32,2048]{1,0:T(8,128)} %get-tuple-element.19.cs_ref, f32[32,2048]{1,0:T(8,128)} %get-tuple-element.20.cc_ref, f32[64,2048]{1,0:T(8,128)} %get-tuple-element.21.fs_ref, ...), custom_call_target="tpu_custom_call" | custom-call | flops 4294967296 | bytes 12582912 | tf_op jit(solution)/shard_map/y_first/pallas_call | solution.py:237
  58.2 5.7 %all-to-all-start.1 = ((bf16[4,512,512]{2,1,0:T(8,128)(2,1)}), bf16[4,512,512]{2,1,0:T(8,128)(2,1)S(1)}, u32[]{:S(2)}, u32[]{:S(2)}) async-start(bf16[4,512,512]{2,1,0:T(8,128)(2,1)} %get-tuple-element.24), calls=%async_computation.1 | async-start | bytes 4194304 | tf_op jit(solution)/shard_map/all_to_all | solution.py:434
  63.8 22.6 %gradient_v.1 = (bf16[512,2048]{1,0:T(8,128)(2,1)}, f32[1,1]{1,0:T(1,128)}) custom-call(s32[4,3,256]{2,1,0:T(4,128)} %pad_add_fusion.cell_ref, f32[4,8,256]{2,1,0:T(8,128)} %copy-done.3, f32[512,2,2048]{2,1,0:T(2,128)} %bitcast.49, f32[2,8,2048]{2,1,0:T(8,128)} %pad_bitcast_fusion.1.low_ref, f32[2,8,2048]{2,1,0:T(8,128)} %pad_bitcast_fusion.high_ref), custom_call_target="tpu_custom_call" | custom-call | flops 62914560 | bytes 12582912 | tf_op jit(solution)/shard_map/gradient_v/pallas_call | solution.py:212
  86.4 8.7 %y_forward.1 = bf16[4,512,512]{2,1,0:T(8,128)(2,1)} custom-call(bf16[512,2048]{1,0:T(8,128)(2,1)} %get-tuple-element.26.grad_ref, bf16[2048,2048]{1,0:T(8,128)(2,1)} %get-tuple-element.27.table_ref), custom_call_target="tpu_custom_call" | custom-call | flops 4294967296 | bytes 12582912 | tf_op jit(solution)/shard_map/y_forward/pallas_call | solution.py:260
  95.1 15.7 %all-to-all-done.1.cols_ref = bf16[4,512,512]{2,1,0:T(8,128)(2,1)S(1)} async-done(((bf16[4,512,512]{2,1,0:T(8,128)(2,1)}), bf16[4,512,512]{2,1,0:T(8,128)(2,1)S(1)}, u32[]{:S(2)}, u32[]{:S(2)}) %all-to-all-start.1) | async-done | bytes 2097184 | tf_op jit(solution)/shard_map/all_to_all | solution.py:434
  112.2 4.5 %all-to-all-start.3 = ((bf16[4,512,512]{2,1,0:T(8,128)(2,1)}), bf16[4,512,512]{2,1,0:T(8,128)(2,1)}, u32[]{:S(2)}, u32[]{:S(2)}) async-start(bf16[4,512,512]{2,1,0:T(8,128)(2,1)} %y_forward.1), calls=%async_computation.3 | async-start | bytes 4194304 | tf_op jit(solution)/shard_map/all_to_all | solution.py:434
  117.3 4.4 %multiply_multiply_fusion.lam_x_ref = f32[2048,1]{1,0:T(8,128)} fusion(), kind=kLoop, calls=%fused_computation.2 | loop fusion | flops 10240 | bytes 8192 | tf_op jit(solution)/shard_map/mul | solution.py:44
  121.7 14.8 %x_transforms.2 = (bf16[4,512,512]{2,1,0:T(8,128)(2,1)}, f32[8,512]{1,0:T(8,128)}) custom-call(bf16[4,512,512]{2,1,0:T(8,128)(2,1)} %copy-done.1, bf16[2048,2048]{1,0:T(8,128)(2,1)} %get-tuple-element.27.table_ref, f32[2048,1]{1,0:T(8,128)} %multiply_multiply_fusion.lam_x_ref, f32[1,512]{1,0:T(1,128)} %multiply_multiply_fusion.1.lam_y_ref), custom_call_target="tpu_custom_call" | custom-call | flops 8589934592 | bytes 20971520 | tf_op jit(solution)/shard_map/x_transforms/pallas_call | solution.py:279
  136.5 27.9 %all-to-all-done.3.cols_ref = bf16[4,512,512]{2,1,0:T(8,128)(2,1)} async-done(((bf16[4,512,512]{2,1,0:T(8,128)(2,1)}), bf16[4,512,512]{2,1,0:T(8,128)(2,1)}, u32[]{:S(2)}, u32[]{:S(2)}) %all-to-all-start.3) | async-done | bytes 2097184 | tf_op jit(solution)/shard_map/all_to_all | solution.py:434
  164.5 3.6 %all-to-all-start.2 = ((bf16[4,512,512]{2,1,0:T(8,128)(2,1)}), bf16[4,512,512]{2,1,0:T(8,128)(2,1)S(1)}, u32[]{:S(2)}, u32[]{:S(2)}) async-start(bf16[4,512,512]{2,1,0:T(8,128)(2,1)} %get-tuple-element.29), calls=%async_computation.2 | async-start | bytes 4194304 | tf_op jit(solution)/shard_map/all_to_all | solution.py:434
  168.1 14.9 %x_transforms.3 = (bf16[4,512,512]{2,1,0:T(8,128)(2,1)}, f32[8,512]{1,0:T(8,128)}) custom-call(bf16[4,512,512]{2,1,0:T(8,128)(2,1)} %all-to-all-done.3.cols_ref, bf16[2048,2048]{1,0:T(8,128)(2,1)} %get-tuple-element.27.table_ref, f32[2048,1]{1,0:T(8,128)} %multiply_multiply_fusion.lam_x_ref, f32[1,512]{1,0:T(1,128)} %multiply_multiply_fusion.1.lam_y_ref), custom_call_target="tpu_custom_call" | custom-call | flops 8589934592 | bytes 20971520 | tf_op jit(solution)/shard_map/x_transforms/pallas_call | solution.py:279
  182.9 32.8 %all-to-all-done.2.rows_ref = bf16[4,512,512]{2,1,0:T(8,128)(2,1)S(1)} async-done(((bf16[4,512,512]{2,1,0:T(8,128)(2,1)}), bf16[4,512,512]{2,1,0:T(8,128)(2,1)S(1)}, u32[]{:S(2)}, u32[]{:S(2)}) %all-to-all-start.2) | async-done | bytes 2097184 | tf_op jit(solution)/shard_map/all_to_all | solution.py:434
  215.7 1.4 copy-done.2
  217.1 3.6 %all-to-all-start.4 = ((bf16[4,512,512]{2,1,0:T(8,128)(2,1)}), bf16[4,512,512]{2,1,0:T(8,128)(2,1)S(1)}, u32[]{:S(2)}, u32[]{:S(2)}) async-start(bf16[4,512,512]{2,1,0:T(8,128)(2,1)} %get-tuple-element.34), calls=%async_computation.4 | async-start | bytes 4194304 | tf_op jit(solution)/shard_map/all_to_all | solution.py:434
  224.4 9.4 %y_back.1.other_ref = f32[512,2048]{1,0:T(8,128)} custom-call(bf16[4,512,512]{2,1,0:T(8,128)(2,1)} %copy-done.2, bf16[2048,2048]{1,0:T(8,128)(2,1)} %get-tuple-element.27.table_ref), custom_call_target="tpu_custom_call" | custom-call | flops 4294967296 | bytes 14680064 | tf_op jit(solution)/shard_map/y_back/pallas_call | solution.py:307
  234.3 37.0 %summed.1 = f32[8,128]{1,0:T(8,128)} custom-call(f32[8,128]{1,0:T(8,128)} %iota.59.own_ref), custom_call_target="tpu_custom_call" | custom-call | tf_op jit(solution)/shard_map/summed/pallas_call | solution.py:418
  271.3 1.4 fusion.24
  275.5 15.3 %last.1 = f32[512,2,2048]{2,1,0:T(2,128)} custom-call(f32[1]{0:T(128)} %bitcast.19.step_ref, bf16[4,512,512]{2,1,0:T(8,128)(2,1)} %copy-done, bf16[2048,2048]{1,0:T(8,128)(2,1)} %get-tuple-element.27.table_ref, f32[512,2048]{1,0:T(8,128)} %y_back.1.other_ref, f32[512,2,2048]{2,1,0:T(2,128)} %bitcast.50), custom_call_target="tpu_custom_call" | custom-call | flops 4294967296 | bytes 31457280 | tf_op jit(solution)/shard_map/last/pallas_call | solution.py:348
  (44 shorter events, 15.2 us)
Async XLA Ops:
  9.6 19.0 %all-to-all-start = ((f32[4,8,256]{2,1,0:T(8,128)}), f32[4,8,256]{2,1,0:T(8,128)S(1)}, u32[]{:S(2)}, u32[]{:S(2)}) async-start(f32[4,8,256]{2,1,0:T(8,128)} %concatenate.9), calls=%async_computation | async-start | bytes 65536 | tf_op jit(solution)/shard_map/all_to_all | solution.py:434
  16.7 11.2 %collective-permute-start = (f32[2,2,2048]{2,0,1:T(2,128)S(1)}, f32[2,2,2048]{2,0,1:T(2,128)S(1)}, u32[]{:S(2)}, u32[]{:S(2)}) collective-permute-start(f32[2,2,2048]{2,0,1:T(2,128)S(1)} %bitcast.52), channel_id=1, source_target_pairs={{0,4},{4,8},{8,12},{1,5},{5,9},{9,13},{2,6},{6,10},{10,14},{3,7},{... | collective-permute-start | bytes 98312 | tf_op jit(solution)/shard_map/ppermute | solution.py:473
  20.7 6.6 %collective-permute-start.1 = (f32[2,2,2048]{2,0,1:T(2,128)S(1)}, f32[2,2,2048]{2,0,1:T(2,128)S(1)}, u32[]{:S(2)}, u32[]{:S(2)}) collective-permute-start(f32[2,2,2048]{2,0,1:T(2,128)S(1)} %bitcast.53), channel_id=1, source_target_pairs={{4,0},{8,4},{12,8},{5,1},{9,5},{13,9},{6,2},{10,6},{14,10},{7,3},{... | collective-permute-start | bytes 98312 | tf_op jit(solution)/shard_map/ppermute | solution.py:474
  28.6 0.7 copy-start.3
  58.2 52.7 %all-to-all-start.1 = ((bf16[4,512,512]{2,1,0:T(8,128)(2,1)}), bf16[4,512,512]{2,1,0:T(8,128)(2,1)S(1)}, u32[]{:S(2)}, u32[]{:S(2)}) async-start(bf16[4,512,512]{2,1,0:T(8,128)(2,1)} %get-tuple-element.24), calls=%async_computation.1 | async-start | bytes 4194304 | tf_op jit(solution)/shard_map/all_to_all | solution.py:434
  110.9 1.3 copy-start.1
  112.2 52.3 %all-to-all-start.3 = ((bf16[4,512,512]{2,1,0:T(8,128)(2,1)}), bf16[4,512,512]{2,1,0:T(8,128)(2,1)}, u32[]{:S(2)}, u32[]{:S(2)}) async-start(bf16[4,512,512]{2,1,0:T(8,128)(2,1)} %y_forward.1), calls=%async_computation.3 | async-start | bytes 4194304 | tf_op jit(solution)/shard_map/all_to_all | solution.py:434
  164.5 51.3 %all-to-all-start.2 = ((bf16[4,512,512]{2,1,0:T(8,128)(2,1)}), bf16[4,512,512]{2,1,0:T(8,128)(2,1)S(1)}, u32[]{:S(2)}, u32[]{:S(2)}) async-start(bf16[4,512,512]{2,1,0:T(8,128)(2,1)} %get-tuple-element.29), calls=%async_computation.2 | async-start | bytes 4194304 | tf_op jit(solution)/shard_map/all_to_all | solution.py:434
  215.7 1.4 copy-start.2
  215.7 6.2 %copy-start.4 = (f32[8,512]{1,0:T(8,128)S(1)}, f32[8,512]{1,0:T(8,128)}, u32[]{:S(2)}) copy-start(f32[8,512]{1,0:T(8,128)} %get-tuple-element.31) | copy-start | bytes 49156
  215.7 6.9 %copy-start.5 = (f32[8,512]{1,0:T(8,128)S(1)}, f32[8,512]{1,0:T(8,128)}, u32[]{:S(2)}) copy-start(f32[8,512]{1,0:T(8,128)} %get-tuple-element.32) | copy-start | bytes 49156
  217.1 57.0 %all-to-all-start.4 = ((bf16[4,512,512]{2,1,0:T(8,128)(2,1)}), bf16[4,512,512]{2,1,0:T(8,128)(2,1)S(1)}, u32[]{:S(2)}, u32[]{:S(2)}) async-start(bf16[4,512,512]{2,1,0:T(8,128)(2,1)} %get-tuple-element.34), calls=%async_computation.4 | async-start | bytes 4194304 | tf_op jit(solution)/shard_map/all_to_all | solution.py:434
  274.1 1.4 copy-start
